TPU v7x, 32 devices: a whole 2x2x4 slice. The times are simulated.
32 devices in a mesh: seq: 8 (over z, x), rep: 4 (over y, core).
Axes of the slice: x: 2, y: 2, z: 4, core: 2. Of those that a mesh axis runs over, the one named last changes fastest.
Arguments:
- t_query: bfloat16 [4, 1024, 4096], P('rep', 'seq'), may hold values from -45 to 45
- t_key: bfloat16 [4, 1024, 512], P('rep', 'seq'), may hold values from -4 to 4
- t_value: bfloat16 [4, 1024, 512], P('rep', 'seq'), may hold values from -6 to 6
- s_query: bfloat16 [4, 1024, 2048], P('rep', 'seq'), may hold values from -45 to 45
- s_key: bfloat16 [4, 1024, 512], P('rep', 'seq'), may hold values from -4 to 4
- student_value: bfloat16 [4, 1024, 512], P('rep', 'seq'), may hold values from -6 to 6
- student_wo: bfloat16 [2048, 2048], P('seq'), may hold values from -0.125 to 0.125
- projection: bfloat16 [4096, 2048], P('seq'), may hold values from -0.09375 to 0.09375
- doc_ids: int32 [4, 1024], P('rep'), may hold values from 0 to 15, never falling along the last dimension, each value on 1 to 256 neighbouring positions
- span_order: int32 [4, 16], P('rep'), may hold values from 0 to 15, each once within a row
Outputs:
- seq_loss: float32 [4], P('rep')
- d_wo: float32 [2048, 2048], P('seq', 'rep')
- d_query: bfloat16 [4, 1024, 2048], P('rep', 'seq')
- d_key: bfloat16 [4, 1024, 512], P('rep', 'seq')
- d_value: bfloat16 [4, 1024, 512], P('rep', 'seq')
All inputs are finite; a program needn't handle non-finite values.
Results may differ from a plain program's by a relative error of at most 0.018.
The roundings to bfloat16 on the way count: a program that leaves them out, or rounds other values in their place, can miss the bound.
Values may be sent and summed in bfloat16 or wider, within the bound.
A program may use at most 128 MiB of HBM per device.

v0:
```python
import math

import jax
import jax.numpy as jnp
from jax import lax
from jax.sharding import PartitionSpec as P

HEAD_WIDTH = 128


MASKED = -1e30


def stored_positions(order_row, length):
    half_len = length // order_row.shape[0]
    offsets = jnp.arange(half_len, dtype=jnp.int32)
    return (order_row[:, None] * half_len + offsets[None, :]).reshape(length)


def head_attention(queries, key_rows, val_rows, positions, stored_docs):
    length = queries.shape[0]
    row_block = math.gcd(length, 512)
    scaling = 1.0 / math.sqrt(HEAD_WIDTH)

    def one_block(block_id):
        first_row = block_id * row_block
        q_block = lax.dynamic_slice_in_dim(queries, first_row, row_block, 0)
        q_pos = lax.dynamic_slice_in_dim(positions, first_row, row_block, 0)
        q_docs = lax.dynamic_slice_in_dim(stored_docs, first_row, row_block, 0)
        allowed = (q_docs[:, None] == stored_docs[None, :]) & (positions[None, :] <= q_pos[:, None])
        scores = (
            jnp.einsum("qhd,kd->hqk", q_block, key_rows, preferred_element_type=jnp.float32)
            * scaling
        )
        scores = jnp.where(allowed, scores, MASKED)
        maximum = jnp.max(scores, axis=2, keepdims=True)
        weights = jnp.where(allowed, jnp.exp(scores - maximum), 0.0)
        totals = jnp.sum(weights, axis=2, keepdims=True)
        prob_rows = (weights / totals).astype(jnp.bfloat16)
        mixed_rows = jnp.einsum(
            "hqk,kd->qhd", prob_rows, val_rows, preferred_element_type=jnp.float32
        )
        return (prob_rows, mixed_rows.astype(jnp.bfloat16))

    block_ids = jnp.arange(length // row_block, dtype=jnp.int32)
    return lax.map(one_block, block_ids)


def shards(
    t_query,
    t_key,
    t_value,
    s_query,
    s_key,
    student_value,
    student_wo,
    projection,
    doc_ids,
    span_order,
):
    groups = lax.axis_size("seq")
    my_index = lax.axis_index("seq")
    tokens = t_query.shape[1]
    length = tokens * groups
    scaling = 1.0 / math.sqrt(HEAD_WIDTH)
    positions = stored_positions(span_order[0], length)
    stored_docs = jnp.take(doc_ids[0], positions)
    first_own = my_index * tokens
    own_pos = lax.dynamic_slice_in_dim(positions, first_own, tokens, 0)
    own_docs = lax.dynamic_slice_in_dim(stored_docs, first_own, tokens, 0)
    t_heads_all = t_query.shape[2] // HEAD_WIDTH
    t_kv = t_key.shape[2] // HEAD_WIDTH
    t_local = t_heads_all // groups
    t_share = t_heads_all // t_kv
    own_queries = t_query[0].reshape(tokens, t_kv, t_share, HEAD_WIDTH)
    start_state = (
        jnp.full((t_kv, t_share, tokens), MASKED, jnp.float32),
        jnp.zeros((t_kv, t_share, tokens), jnp.float32),
        jnp.zeros((t_kv, t_share, tokens, HEAD_WIDTH), jnp.float32),
    )
    carried = start_state
    key_piece = lax.all_gather(t_key[0], "seq", axis=0, tiled=True)
    val_piece = lax.all_gather(t_value[0], "seq", axis=0, tiled=True)
    row_count = key_piece.shape[0]
    sub_rows = math.gcd(row_count, 512)
    for offset in range(0, row_count, sub_rows):
        key_block = key_piece[offset : offset + sub_rows].reshape(sub_rows, t_kv, HEAD_WIDTH)
        val_block = val_piece[offset : offset + sub_rows].reshape(sub_rows, t_kv, HEAD_WIDTH)
        key_pos = lax.dynamic_slice_in_dim(positions, offset, sub_rows, 0)
        key_docs = lax.dynamic_slice_in_dim(stored_docs, offset, sub_rows, 0)
        allowed = (own_docs[:, None] == key_docs[None, :]) & (key_pos[None, :] <= own_pos[:, None])

        def absorb(states):
            running_max, running_sum, accumulated = states
            scores = (
                jnp.einsum(
                    "tkgd,skd->kgts", own_queries, key_block, preferred_element_type=jnp.float32
                )
                * scaling
            )
            scores = jnp.where(allowed, scores, MASKED)
            new_max = jnp.maximum(running_max, jnp.max(scores, axis=3))
            weights = jnp.where(allowed, jnp.exp(scores - new_max[..., None]), 0.0)
            factor = jnp.exp(running_max - new_max)
            running_sum = running_sum * factor + jnp.sum(weights, axis=3)
            accumulated = accumulated * factor[..., None] + jnp.einsum(
                "kgts,skd->kgtd",
                weights.astype(jnp.bfloat16),
                val_block,
                preferred_element_type=jnp.float32,
            )
            return (new_max, running_sum, accumulated)

        carried = lax.cond(jnp.any(allowed), absorb, lambda unchanged: unchanged, carried)
    running_max, running_sum, accumulated = carried
    teacher_rows = (accumulated / running_sum[..., None]).astype(jnp.bfloat16)
    teacher_rows = jnp.transpose(teacher_rows, (2, 0, 1, 3)).reshape(
        tokens, groups, t_local * HEAD_WIDTH
    )
    teacher_out = lax.all_to_all(
        teacher_rows, "seq", split_axis=1, concat_axis=0, tiled=True
    ).reshape(length, t_local * HEAD_WIDTH)
    s_heads_all = s_query.shape[2] // HEAD_WIDTH
    s_local = s_heads_all // groups
    s_kv = s_key.shape[2] // HEAD_WIDTH
    student_rows = s_query[0].reshape(tokens, groups, s_local * HEAD_WIDTH)
    student_heads = lax.all_to_all(student_rows, "seq", split_axis=1, concat_axis=0, tiled=True)
    all_keys, all_values = (
        lax.all_gather(s_key[0], "seq", axis=0, tiled=True),
        lax.all_gather(student_value[0], "seq", axis=0, tiled=True),
    )
    kv_index = my_index // (groups // s_kv)
    key_heads = lax.dynamic_slice_in_dim(all_keys, kv_index * HEAD_WIDTH, HEAD_WIDTH, 1)
    val_heads = lax.dynamic_slice_in_dim(all_values, kv_index * HEAD_WIDTH, HEAD_WIDTH, 1)
    student_heads = student_heads.reshape(length, s_local, HEAD_WIDTH)
    prob_blocks, student_blocks = head_attention(
        student_heads, key_heads, val_heads, positions, stored_docs
    )
    student_out = student_blocks.reshape(length, s_local * HEAD_WIDTH)
    width_all = student_wo.shape[1]
    own_diff = lax.psum_scatter(
        (
            jnp.dot(student_out, student_wo, preferred_element_type=jnp.float32)
            - jnp.dot(teacher_out, projection, preferred_element_type=jnp.float32)
        ).astype(jnp.bfloat16),
        "seq",
        scatter_dimension=0,
        tiled=True,
    ).astype(jnp.float32)
    squares = lax.psum(jnp.sum(own_diff * own_diff), "seq")
    seq_loss = (squares / (length * width_all)).reshape(1)
    own_grad = own_diff.astype(jnp.bfloat16)
    piece_rows = lax.all_gather(own_grad, "seq", axis=0, tiled=True)
    attn_rows = jnp.einsum("rc,hc->rh", piece_rows, student_wo, preferred_element_type=jnp.float32)
    d_attn = attn_rows
    d_weight = jnp.einsum("rh,rc->hc", student_out, piece_rows, preferred_element_type=jnp.float32)
    d_attn, d_weight = (d_attn, d_weight)
    row_block = math.gcd(length, 512)
    blocks = length // row_block
    grad_blocks = d_attn.astype(jnp.bfloat16).reshape(blocks, row_block, s_local, HEAD_WIDTH)
    query_blocks = student_heads.reshape(blocks, row_block, s_local, HEAD_WIDTH)

    def back_block(carried, inputs):
        d_key, d_value = carried
        prob_block, out_block, grad_block, query_block = inputs
        row_delta = jnp.sum(grad_block.astype(jnp.float32) * out_block.astype(jnp.float32), axis=2)
        d_value = d_value + jnp.einsum(
            "hqk,qhd->kd", prob_block, grad_block, preferred_element_type=jnp.float32
        )
        d_prob = jnp.einsum(
            "qhd,kd->hqk", grad_block, val_heads, preferred_element_type=jnp.float32
        )
        d_score = (
            prob_block.astype(jnp.float32) * (d_prob - jnp.transpose(row_delta)[:, :, None])
        ).astype(jnp.bfloat16)
        d_query = (
            jnp.einsum("hqk,kd->qhd", d_score, key_heads, preferred_element_type=jnp.float32)
            * scaling
        ).astype(jnp.bfloat16)
        d_key = d_key + jnp.einsum(
            "hqk,qhd->kd", d_score, query_block, preferred_element_type=jnp.float32
        )
        return ((d_key, d_value), d_query)

    zero_rows = jnp.zeros((length, HEAD_WIDTH), jnp.float32)
    (d_key, d_value), d_query = lax.scan(
        back_block, (zero_rows, zero_rows), (prob_blocks, student_blocks, grad_blocks, query_blocks)
    )
    query_part = d_query.reshape(length, 1, s_local * HEAD_WIDTH)
    key_part = (d_key * scaling).astype(jnp.bfloat16).reshape(length, 1, HEAD_WIDTH)
    value_part = d_value.astype(jnp.bfloat16).reshape(length, 1, HEAD_WIDTH)
    back_query, back_key, back_value = (
        lax.all_to_all(query_part, "seq", split_axis=0, concat_axis=1, tiled=True),
        lax.all_to_all(key_part, "seq", split_axis=0, concat_axis=1, tiled=True),
        lax.all_to_all(value_part, "seq", split_axis=0, concat_axis=1, tiled=True),
    )
    repeat_count = groups // s_kv

    def merge_slots(slot_rows):
        summed = (
            slot_rows.reshape(tokens, s_kv, repeat_count, HEAD_WIDTH)
            .astype(jnp.float32)
            .sum(axis=2)
        )
        return summed.astype(jnp.bfloat16).reshape(1, tokens, s_kv * HEAD_WIDTH)

    weight_share = lax.psum_scatter(
        d_weight.astype(jnp.bfloat16), "rep", scatter_dimension=1, tiled=True
    ).astype(jnp.float32)
    return (
        seq_loss,
        weight_share,
        back_query.reshape(1, tokens, s_heads_all * HEAD_WIDTH),
        merge_slots(back_key),
        merge_slots(back_value),
    )


def solution(mesh):
    in_specs = (
        P("rep", "seq", None),
        P("rep", "seq", None),
        P("rep", "seq", None),
        P("rep", "seq", None),
        P("rep", "seq", None),
        P("rep", "seq", None),
        P("seq", None),
        P("seq", None),
        P("rep", None),
        P("rep", None),
    )
    out_specs = (
        P("rep"),
        P("seq", "rep"),
        P("rep", "seq", None),
        P("rep", "seq", None),
        P("rep", "seq", None),
    )
    return jax.shard_map(shards, mesh=mesh, in_specs=in_specs, out_specs=out_specs, check_vma=False)
```

profile of v0, /device:TPU:11, one launch (start us, length us, event | category | flops | bytes accessed | tf_op | source)
XLA Modules:
  0.0 476.4 jit_solution(237387720823039704)
XLA Ops:
  7.2 1.8 copy.103
  9.1 1.7 copy.105
  13.6 5.7 %all-to-all-start = ((bf16[128,8,256]{2,0,1:T(8,128)(2,1)}), bf16[128,8,256]{2,0,1:T(8,128)(2,1)}, u32[]{:S(2)}, u32[]{:S(2)}) async-start(bf16[128,8,256]{2,0,1:T(8,128)(2,1)} %copy.99), calls=%async_computation | async-start | bytes 1048576 | tf_op jit(solution)/shard_map/all_to_all | solution.py:127
  20.2 4.5 gather_fusion
  27.3 1.6 copy.104
  29.0 6.5 %all-to-all-done = bf16[128,8,256]{2,0,1:T(8,128)(2,1)} async-done(((bf16[128,8,256]{2,0,1:T(8,128)(2,1)}), bf16[128,8,256]{2,0,1:T(8,128)(2,1)}, u32[]{:S(2)}, u32[]{:S(2)}) %all-to-all-start) | async-done | bytes 524320 | tf_op jit(solution)/shard_map/all_to_all | solution.py:127
  35.4 2.0 reshape.193
  37.4 17.6 %all-gather.16.cloned.1.call-done = bf16[1,1024,512]{1,2,0:T(8,128)(2,1)} async-done(((bf16[1,128,512]{1,2,0:T(8,128)(2,1)}), bf16[1,1024,512]{1,2,0:T(8,128)(2,1)}) %all-gather.16.cloned.1.call-update) | async-done | bytes 1048592 | tf_op jit(solution)/shard_map/all_gather | solution.py:82
  55.0 41.1 %all-gather.18.cloned.1.call-done = bf16[1,1024,512]{1,2,0:T(8,128)(2,1)} async-done(((bf16[1,128,512]{1,2,0:T(8,128)(2,1)}), bf16[1,1024,512]{1,2,0:T(8,128)(2,1)}) %all-gather.18.cloned.1.call-update) | async-done | bytes 1048592 | tf_op jit(solution)/shard_map/all_gather | solution.py:83
  96.1 11.3 %conditional.2 = (f32[4,8,128]{2,1,0:T(8,128)}, f32[4,8,128]{2,1,0:T(8,128)S(1)}, f32[4,8,128,128]{3,2,1,0:T(8,128)S(1)}) conditional(s32[]{:T(128)} %convert_element_type.72, () %tuple.32, (pred[128,512]{0,1:T(8,128)(4,1)S(1)}, bf16[1024,512]{0,1:T(8,128)(2,1)}, bf16[128,4,8,128]{0,3,2,1:T(8,128)(2,1)S(1)}, bf16[1024,512]{0,1:T(8,128)(2,1)}) %tuple.134), branch_computations={%region_6.7_spmd, %region_7.10_spmd} | conditional | flops 1101545472 | bytes 31834136 | solution.py:114
  98.3 1.4 fusion.2
  100.3 2.8 fusion.4
  103.1 3.6 fusion.8
  107.4 14.8 %conditional.3 = (f32[4,8,128]{2,1,0:T(8,128)S(1)}, f32[4,8,128,128]{2,3,1,0:T(8,128)}) conditional(s32[]{:T(128)} %convert_element_type.71, (f32[4,8,128]{2,1,0:T(8,128)S(1)}, f32[4,8,128,128]{3,2,1,0:T(8,128)S(1)}) %tuple.34, (pred[128,512]{0,1:T(8,128)(4,1)S(1)}, bf16[1024,512]{0,1:T(8,128)(2,1)}, bf16[128,4,8,128]{0,3,2,1:T(8,128)(2,1)S(1)}, ...), branch_computations={%region_10.11_spmd, %region_11.14_spmd} | conditional | flops 1102061568 | bytes 54952008 | solution.py:114
  107.6 1.5 slice.17
  110.2 1.4 fusion.15
  112.4 2.2 fusion.17
  115.3 4.1 multiply_add_fusion
  119.4 2.9 copy.143
  122.3 2.9 divide_convert_fusion.1
  125.1 5.4 %all-to-all-start.1 = ((bf16[128,8,512]{0,2,1:T(8,128)(2,1)}), bf16[128,8,512]{0,2,1:T(8,128)(2,1)}, u32[]{:S(2)}, u32[]{:S(2)}) async-start(bf16[128,8,512]{0,2,1:T(8,128)(2,1)} %bitcast.21), calls=%async_computation.1 | async-start | bytes 2097152 | tf_op jit(solution)/shard_map/all_to_all | solution.py:120
  130.5 10.1 %all-gather.12.cloned.1.call-done = bf16[1,1024,512]{2,1,0:T(8,128)(2,1)} async-done(((bf16[1,128,512]{2,1,0:T(8,128)(2,1)}), bf16[1,1024,512]{2,1,0:T(8,128)(2,1)}) %all-gather.12.cloned.1.call-update) | async-done | bytes 1048592 | tf_op jit(solution)/shard_map/all_gather | solution.py:129
  141.5 42.6 %all-gather.14.cloned.1.call-done = bf16[1,1024,512]{2,1,0:T(8,128)(2,1)} async-done(((bf16[1,128,512]{2,1,0:T(8,128)(2,1)}), bf16[1,1024,512]{2,1,0:T(8,128)(2,1)}) %all-gather.14.cloned.1.call-update) | async-done | bytes 1048592 | tf_op jit(solution)/shard_map/all_gather | solution.py:130
  185.2 26.0 %while.28 = (s32[]{:T(128)}, bf16[2,2,512,1024]{3,2,1,0:T(8,128)(2,1)}, bf16[2,512,2,128]{3,1,2,0:T(8,128)(2,1)}, s32[2]{0:T(128)S(1)}, s32[1024]{0:T(1024)S(1)}...) while((s32[]{:T(128)}, ...), condition=%wide.region_3.4_spmd.clone, body=%wide.region_0.3_spmd.clone.sunk | while | flops 545916928 | bytes 21537108 | solution.py:46
  188.3 4.1 fusion.125
  192.4 4.2 bitcast_dynamic-update-slice_fusion.2
  201.4 4.1 fusion.125
  205.4 4.1 bitcast_dynamic-update-slice_fusion.2
  211.2 1.6 copy.102
  212.8 2.5 copy.109
  215.3 3.6 fusion.89
  218.9 3.3 subtract_convert_fusion
  222.3 89.4 %reduce-scatter.3.cloned.1.call-done = bf16[128,2048]{1,0:T(8,128)(2,1)} async-done(((bf16[1024,2048]{1,0:T(8,128)(2,1)}), bf16[128,2048]{1,0:T(8,128)(2,1)}) %reduce-scatter.3.cloned.1.call-update) | async-done | bytes 524304 | tf_op jit(solution)/shard_map/reduce_scatter | solution.py:141
  313.2 71.2 %all-gather.10.cloned.1.call-done = bf16[1024,2048]{1,0:T(8,128)(2,1)} async-done(((bf16[128,2048]{1,0:T(8,128)(2,1)}), bf16[1024,2048]{1,0:T(8,128)(2,1)}) %all-gather.10.cloned.1.call-update) | async-done | bytes 4194320 | tf_op jit(solution)/shard_map/all_gather | solution.py:153
  384.4 3.8 convolution_convert_fusion.2
  388.3 13.4 %while.29 = (s32[]{:T(128)}, f32[1024,128]{1,0:T(8,128)S(1)}, f32[1024,128]{1,0:T(8,128)}, bf16[2,512,2,128]{3,2,1,0:T(2,128)(2,1)}, bf16[2,2,512,1024]{3,2,1,0:...) while((s32[]{:T(128)}, f32[1024,128]{1,0:T(8,128)S(1)}, ...), condition=%wide.region_20.21_spmd.clone, body=%wide.region_18.20_spmd.clone.sunk | while | flops 1079245824 | bytes 37232876 | solution.py:186
  388.7 3.4 fusion.136
  395.4 3.5 fusion.136
  401.7 4.6 convolution_convert_fusion.1
  408.6 5.6 %all-to-all-start.3 = ((bf16[8,2,8192]{2,1,0:T(2,128)(2,1)}), bf16[8,2,8192]{2,1,0:T(2,128)(2,1)S(1)}, u32[]{:S(2)}, u32[]{:S(2)}) async-start(bf16[8,2,8192]{2,1,0:T(2,128)(2,1)} %reshape.197), calls=%async_computation.5 | async-start | bytes 524288 | tf_op jit(solution)/shard_map/all_to_all | solution.py:194
  415.8 4.1 all-to-all-done.3
  419.9 6.4 %all-to-all-start.4 = ((bf16[8,2,8192]{2,1,0:T(2,128)(2,1)}), bf16[8,2,8192]{2,1,0:T(2,128)(2,1)S(1)}, u32[]{:S(2)}, u32[]{:S(2)}) async-start(bf16[8,2,8192]{2,1,0:T(2,128)(2,1)} %reshape.199), calls=%async_computation.6 | async-start | bytes 524288 | tf_op jit(solution)/shard_map/all_to_all | solution.py:195
  426.5 3.8 reduce.2
  432.0 6.2 %all-to-all-start.2 = ((bf16[8,2,16384]{2,1,0:T(2,128)(2,1)}), bf16[8,2,16384]{2,1,0:T(2,128)(2,1)}, u32[]{:S(2)}, u32[]{:S(2)}) async-start(bf16[8,2,16384]{2,1,0:T(2,128)(2,1)} %reshape.195), calls=%async_computation.4 | async-start | bytes 1048576 | tf_op jit(solution)/shard_map/all_to_all | solution.py:193
  439.1 18.8 %psum.7 = f32[]{:T(128)} all-reduce(f32[]{:T(128)} %multiply_reduce_fusion), channel_id=1, replica_groups=mesh['seq'=8,'rep'=4] {'seq'}, use_global_device_ids=true, to_apply=%region_16.17 | all-reduce | flops 1 | bytes 8 | tf_op jit(solution)/shard_map/psum | solution.py:150
  461.2 2.2 reshape.196
  464.3 1.3 copy.114
  466.6 1.8 convert_element_type.77
  (144 shorter events, 40.3 us)
Async XLA Ops:
  7.2 208.1 %copy-start = (bf16[512,2048]{1,0:T(8,128)(2,1)S(1)}, bf16[512,2048]{1,0:T(8,128)(2,1)}, u32[]{:S(2)}) copy-start(bf16[512,2048]{1,0:T(8,128)(2,1)} %param.25) | copy-start | bytes 6291460
  7.2 12.7 %copy-start.17 = (s32[1,16]{1,0:T(1,128)S(1)}, s32[1,16]{1,0:T(1,128)}, u32[]{:S(2)}) copy-start(s32[1,16]{1,0:T(1,128)} %param.27) | copy-start | bytes 196
  7.2 13.0 %copy-start.2 = (s32[1,1024]{1,0:T(1,128)S(1)}, s32[1,1024]{1,0:T(1,128)}, u32[]{:S(2)}) copy-start(s32[1,1024]{1,0:T(1,128)} %param.26) | copy-start | bytes 12292
  7.2 47.8 %all-gather.16.cloned.1.call-start = ((), (), s32[]{:S(2)}) async-start(), calls=%async_computation.12 | async-start | bytes 1179648 | tf_op jit(solution)/shard_map/all_gather | solution.py:82
  9.1 87.1 %all-gather.18.cloned.1.call-start = ((), (), s32[]{:S(2)}) async-start(), calls=%async_computation.13 | async-start | bytes 1179648 | tf_op jit(solution)/shard_map/all_gather | solution.py:83
  10.8 129.8 %all-gather.12.cloned.1.call-start = ((), (), s32[]{:S(2)}) async-start(), calls=%async_computation.10 | async-start | bytes 1179648 | tf_op jit(solution)/shard_map/all_gather | solution.py:129
  13.6 21.8 %all-to-all-start = ((bf16[128,8,256]{2,0,1:T(8,128)(2,1)}), bf16[128,8,256]{2,0,1:T(8,128)(2,1)}, u32[]{:S(2)}, u32[]{:S(2)}) async-start(bf16[128,8,256]{2,0,1:T(8,128)(2,1)} %copy.99), calls=%async_computation | async-start | bytes 1048576 | tf_op jit(solution)/shard_map/all_to_all | solution.py:127
  19.3 164.9 %all-gather.14.cloned.1.call-start = ((), (), s32[]{:S(2)}) async-start(), calls=%async_computation.11 | async-start | bytes 1179648 | tf_op jit(solution)/shard_map/all_gather | solution.py:130
  107.6 2.6 copy-start.5
  112.4 2.9 copy-start.6
  125.1 87.6 %all-to-all-start.1 = ((bf16[128,8,512]{0,2,1:T(8,128)(2,1)}), bf16[128,8,512]{0,2,1:T(8,128)(2,1)}, u32[]{:S(2)}, u32[]{:S(2)}) async-start(bf16[128,8,512]{0,2,1:T(8,128)(2,1)} %bitcast.21), calls=%async_computation.1 | async-start | bytes 2097152 | tf_op jit(solution)/shard_map/all_to_all | solution.py:120
  130.5 181.1 %reduce-scatter.3.cloned.1.call-start = ((), (), s32[]{:S(2)}) async-start(), calls=%async_computation.7 | async-start | bytes 4718592 | tf_op jit(solution)/shard_map/reduce_scatter | solution.py:141
  192.4 4.2 copy-start.7
  197.4 0.8 copy-start.8
  205.4 4.1 copy-start.7
  210.4 0.8 copy-start.8
  212.8 6.1 %copy-start.10 = (bf16[2,512,2,128]{3,2,1,0:T(2,128)(2,1)}, bf16[2,512,2,128]{3,2,1,0:T(2,128)(2,1)S(1)}, u32[]{:S(2)}) copy-start(bf16[2,512,2,128]{3,2,1,0:T(2,128)(2,1)S(1)} %copy.102) | copy-start | bytes 1572868
  215.3 3.7 copy-start.12
  222.2 162.1 %all-gather.10.cloned.1.call-start = ((), (), s32[]{:S(2)}) async-start(), calls=%async_computation.8 | async-start | bytes 4718592 | tf_op jit(solution)/shard_map/all_gather | solution.py:153
  311.7 155.0 %reduce-scatter.5.cloned.1.call-start = ((), (), s32[]{:S(2)}) async-start(), calls=%async_computation.9 | async-start | bytes 1310720 | tf_op jit(solution)/shard_map/reduce_scatter | solution.py:207
  313.2 75.1 %copy-start.9 = (bf16[2,512,2,128]{3,1,2,0:T(8,128)(2,1)S(1)}, bf16[2,512,2,128]{3,1,2,0:T(8,128)(2,1)}, u32[]{:S(2)}) copy-start(bf16[2,512,2,128]{3,1,2,0:T(8,128)(2,1)} %get-tuple-element.639) | copy-start | bytes 1572868
  388.3 3.8 copy-start.3
  392.1 1.4 copy-start.13
  394.1 0.9 copy-start.14
  395.0 3.9 copy-start.3
  398.9 1.4 copy-start.13
  400.8 0.9 copy-start.14
  401.7 4.7 copy-start.16
  406.3 19.9 %copy-start.15 = (bf16[2,512,2,128]{3,2,1,0:T(2,128)(2,1)S(1)}, bf16[2,512,2,128]{3,2,1,0:T(2,128)(2,1)}, u32[]{:S(2)}) copy-start(bf16[2,512,2,128]{3,2,1,0:T(2,128)(2,1)} %get-tuple-element.169) | copy-start | bytes 1572868
  407.0 31.3 %copy-start.11 = (bf16[128,2048]{1,0:T(8,128)(2,1)S(1)}, bf16[128,2048]{1,0:T(8,128)(2,1)}, u32[]{:S(2)}) copy-start(bf16[128,2048]{1,0:T(8,128)(2,1)} %reduce-scatter.3.cloned.1.call-done) | copy-start | bytes 1572868
  408.6 11.3 %all-to-all-start.3 = ((bf16[8,2,8192]{2,1,0:T(2,128)(2,1)}), bf16[8,2,8192]{2,1,0:T(2,128)(2,1)S(1)}, u32[]{:S(2)}, u32[]{:S(2)}) async-start(bf16[8,2,8192]{2,1,0:T(2,128)(2,1)} %reshape.197), calls=%async_computation.5 | async-start | bytes 524288 | tf_op jit(solution)/shard_map/all_to_all | solution.py:194
  419.9 12.2 %all-to-all-start.4 = ((bf16[8,2,8192]{2,1,0:T(2,128)(2,1)}), bf16[8,2,8192]{2,1,0:T(2,128)(2,1)S(1)}, u32[]{:S(2)}, u32[]{:S(2)}) async-start(bf16[8,2,8192]{2,1,0:T(2,128)(2,1)} %reshape.199), calls=%async_computation.6 | async-start | bytes 524288 | tf_op jit(solution)/shard_map/all_to_all | solution.py:195
  432.0 29.2 %all-to-all-start.2 = ((bf16[8,2,16384]{2,1,0:T(2,128)(2,1)}), bf16[8,2,16384]{2,1,0:T(2,128)(2,1)}, u32[]{:S(2)}, u32[]{:S(2)}) async-start(bf16[8,2,16384]{2,1,0:T(2,128)(2,1)} %reshape.195), calls=%async_computation.4 | async-start | bytes 1048576 | tf_op jit(solution)/shard_map/all_to_all | solution.py:193
  459.1 9.3 %copy-start.1 = (bf16[512,2048]{1,0:T(8,128)(2,1)S(1)}, bf16[512,2048]{1,0:T(8,128)(2,1)}, u32[]{:S(2)}) copy-start(bf16[512,2048]{1,0:T(8,128)(2,1)} %param.25) | copy-start | bytes 6291460
Sparse Core Ops, SparseCore 0:
  10.7 44.3 all-gather.15
  57.7 38.4 all-gather.17
  98.3 42.2 all-gather.11
  142.5 41.5 all-gather.13
  222.3 89.2 reduce-scatter.2
  313.8 70.4 all-gather.9
  406.5 25.7 reduce-scatter.4
where the time goes:
time: 484 us; the launch traced here: 476 us
  waiting for transfers between devices  285 us (59%)
  matrix products  47 us (10%)
  local copies, waits for them, and re-layouts  46.9 us (10%)
  other arithmetic  30 us (6%)
  starting transfers between devices  29.7 us (6%)
  blocking collectives  18.8 us (4%)
  between operations  17.6 us (4%)
    reduce_scatter x1, waiting for transfers between devices, shards(): lax.psum_scatter((jnp.dot(student_out, student_wo, preferred_element_type...  89.4 us
    all_gather x1, waiting for transfers between devices, shards(): piece_rows = lax.all_gather(own_grad, 'seq', axis=0, tiled=True)  71.2 us
    all_gather x1, waiting for transfers between devices, shards(): lax.all_gather(student_value[0], 'seq', axis=0, tiled=True)  42.6 us
    all_gather x1, waiting for transfers between devices, shards(): val_piece = lax.all_gather(t_value[0], 'seq', axis=0, tiled=True)  41.1 us
    psum x1, blocking collectives, shards(): squares = lax.psum(jnp.sum(own_diff * own_diff), 'seq')  18.8 us
    all_gather x1, waiting for transfers between devices, shards(): key_piece = lax.all_gather(t_key[0], 'seq', axis=0, tiled=True)  17.6 us
    unnamed x36, local copies, waits for them, and re-layouts  15 us
    all_gather x1, waiting for transfers between devices, shards(): lax.all_gather(s_key[0], 'seq', axis=0, tiled=True)  10.1 us
  transfers between devices with their start and end apart: 12, of which 9 were waited for; matrix products, arithmetic and copies ran while one was open for 18% of the time, Pallas kernels for 0%

commit v1 on v0

v1 whole, which is shorter than its diff:
```python
import functools
import math

import jax
import jax.numpy as jnp
from jax import lax
from jax.experimental import pallas as pl
from jax.experimental.pallas import tpu as pltpu
from jax.sharding import PartitionSpec as P

HEAD_WIDTH = 128
ROWS = 128
MASKED = -1e30
VMEM_LIMIT = 48 * 1024 * 1024
NT = (((1,), (1,)), ((), ()))
TN = (((0,), (0,)), ((), ()))


def windows(length):
    reach = length // 4
    out = []
    for first in range(0, length, ROWS):
        out.append((first, max(0, first - reach), first + ROWS))
    return out


def to_true_order(inverse_ref, source_ref, target_ref, halves, half):
    for place in range(halves):
        start = pl.multiple_of(inverse_ref[place] * half, half)
        target_ref[place * half : (place + 1) * half, :] = source_ref[pl.ds(start, half), :]


def block_weights(heads, queries, keys, doc_col, doc_row, first, low, high):
    scores = lax.dot_general(queries, keys, NT, preferred_element_type=jnp.float32)
    row_id = lax.broadcasted_iota(jnp.int32, (ROWS, high - low), 0) + first
    col_id = lax.broadcasted_iota(jnp.int32, (ROWS, high - low), 1) + low
    allowed = (doc_col == doc_row) & (col_id <= row_id)
    scores = scores.reshape(heads, ROWS, high - low)
    scores = jnp.where(allowed[None], scores, MASKED)
    top = jnp.max(scores, axis=2, keepdims=True)
    rate = 1.4426950408889634 / math.sqrt(HEAD_WIDTH)
    weights = jnp.exp2((scores - top) * rate)
    totals = jnp.sum(weights, axis=2, keepdims=True)
    return weights, totals


def stacked(ref, heads, first, last):
    return jnp.concatenate(
        [ref[first:last, h * HEAD_WIDTH : (h + 1) * HEAD_WIDTH] for h in range(heads)], axis=0
    )


def teacher_kernel(heads, halves, inverse_ref, pack_ref, col_ref, row_ref, out_ref, held):
    length = pack_ref.shape[0]
    to_true_order(inverse_ref, pack_ref, held, halves, length // halves)
    at = heads * HEAD_WIDTH
    for first, low, high in windows(length):
        queries = stacked(held, heads, first, first + ROWS)
        weights, totals = block_weights(
            heads, queries, held[low:high, at : at + HEAD_WIDTH],
            col_ref[first : first + ROWS, :], row_ref[:, low:high], first, low, high,
        )
        mixed = jnp.dot(
            weights.astype(jnp.bfloat16).reshape(heads * ROWS, high - low),
            held[low:high, at + HEAD_WIDTH : at + 2 * HEAD_WIDTH],
            preferred_element_type=jnp.float32,
        ).reshape(heads, ROWS, HEAD_WIDTH)
        mixed = (mixed / totals).astype(jnp.bfloat16)
        for h in range(heads):
            out_ref[first : first + ROWS, h * HEAD_WIDTH : (h + 1) * HEAD_WIDTH] = mixed[h]


def student_kernel(heads, halves, inverse_ref, pack_ref, col_ref, row_ref, out_ref, held, prob_ref):
    length = pack_ref.shape[0]
    to_true_order(inverse_ref, pack_ref, held, halves, length // halves)
    at = heads * HEAD_WIDTH
    for i, (first, low, high) in enumerate(windows(length)):
        queries = stacked(held, heads, first, first + ROWS)
        weights, totals = block_weights(
            heads, queries, held[low:high, at : at + HEAD_WIDTH],
            col_ref[first : first + ROWS, :], row_ref[:, low:high], first, low, high,
        )
        probs = (weights / totals).astype(jnp.bfloat16).reshape(heads * ROWS, high - low)
        prob_ref[i, :, : high - low] = probs
        mixed = jnp.dot(
            probs, held[low:high, at + HEAD_WIDTH : at + 2 * HEAD_WIDTH],
            preferred_element_type=jnp.float32,
        ).astype(jnp.bfloat16)
        for h in range(heads):
            out_ref[first : first + ROWS, h * HEAD_WIDTH : (h + 1) * HEAD_WIDTH] = mixed[
                h * ROWS : (h + 1) * ROWS
            ]


def back_kernel(heads, halves, order_ref, held_ref, prob_ref, so_ref, grad_ref, out_ref, done, dk, dv):
    length = held_ref.shape[0]
    half = length // halves
    at = heads * HEAD_WIDTH
    scaling = 1.0 / math.sqrt(HEAD_WIDTH)
    dk[...] = jnp.zeros_like(dk)
    dv[...] = jnp.zeros_like(dv)
    for i, (first, low, high) in enumerate(windows(length)):
        queries = stacked(held_ref, heads, first, first + ROWS)
        grads = stacked(grad_ref, heads, first, first + ROWS)
        outs = stacked(so_ref, heads, first, first + ROWS)
        probs = prob_ref[i, :, : high - low]
        delta = jnp.sum(
            grads.astype(jnp.float32) * outs.astype(jnp.float32), axis=1, keepdims=True
        )
        d_prob = lax.dot_general(
            grads, held_ref[low:high, at + HEAD_WIDTH : at + 2 * HEAD_WIDTH], NT,
            preferred_element_type=jnp.float32,
        )
        d_score = (probs.astype(jnp.float32) * (d_prob - delta)).astype(jnp.bfloat16)
        d_query = (
            jnp.dot(
                d_score, held_ref[low:high, at : at + HEAD_WIDTH],
                preferred_element_type=jnp.float32,
            )
            * scaling
        ).astype(jnp.bfloat16)
        for h in range(heads):
            done[first : first + ROWS, h * HEAD_WIDTH : (h + 1) * HEAD_WIDTH] = d_query[
                h * ROWS : (h + 1) * ROWS
            ]
        dk[low:high, :] += lax.dot_general(d_score, queries, TN, preferred_element_type=jnp.float32)
        dv[low:high, :] += lax.dot_general(probs, grads, TN, preferred_element_type=jnp.float32)
    done[:, at : at + HEAD_WIDTH] = (dk[...] * scaling).astype(jnp.bfloat16)
    done[:, at + HEAD_WIDTH : at + 2 * HEAD_WIDTH] = dv[...].astype(jnp.bfloat16)
    for place in range(halves):
        start = pl.multiple_of(order_ref[place] * half, half)
        out_ref[place * half : (place + 1) * half, :] = done[pl.ds(start, half), :]


SMEM = pl.BlockSpec(memory_space=pltpu.SMEM)
VMEM = pl.BlockSpec(memory_space=pltpu.VMEM)
PARAMS = pltpu.CompilerParams(vmem_limit_bytes=VMEM_LIMIT)


def shape(dims, dtype=jnp.bfloat16):
    return jax.ShapeDtypeStruct(dims, dtype)


def teacher_attention(heads, halves, inverse, pack, col, row):
    length, wide = pack.shape
    flops = 4 * heads * HEAD_WIDTH * length * (length // 4 + ROWS)
    return pl.pallas_call(
        functools.partial(teacher_kernel, heads, halves),
        out_shape=shape((length, heads * HEAD_WIDTH)),
        in_specs=[SMEM, VMEM, VMEM, VMEM],
        out_specs=VMEM,
        scratch_shapes=[pltpu.VMEM((length, wide), jnp.bfloat16)],
        compiler_params=PARAMS,
        cost_estimate=pl.CostEstimate(flops=flops, bytes_accessed=4 << 20, transcendentals=flops // 512),
        name="teacher_attention",
    )(inverse, pack, col, row)


def student_attention(heads, halves, inverse, pack, col, row):
    length, wide = pack.shape
    flops = 4 * heads * HEAD_WIDTH * length * (length // 4 + ROWS)
    return pl.pallas_call(
        functools.partial(student_kernel, heads, halves),
        out_shape=(
            shape((length, heads * HEAD_WIDTH)),
            shape((length, wide)),
            shape((length // ROWS, heads * ROWS, length // 4 + ROWS)),
        ),
        in_specs=[SMEM, VMEM, VMEM, VMEM],
        out_specs=(VMEM, VMEM, VMEM),
        compiler_params=PARAMS,
        cost_estimate=pl.CostEstimate(flops=flops, bytes_accessed=6 << 20, transcendentals=flops // 512),
        name="student_attention",
    )(inverse, pack, col, row)


def student_backward(heads, halves, order, held, probs, out, grad):
    length, wide = held.shape
    flops = 10 * heads * HEAD_WIDTH * length * (length // 4 + ROWS)
    return pl.pallas_call(
        functools.partial(back_kernel, heads, halves),
        out_shape=shape((length, wide)),
        in_specs=[SMEM, VMEM, VMEM, VMEM, VMEM],
        out_specs=VMEM,
        scratch_shapes=[
            pltpu.VMEM((length, wide), jnp.bfloat16),
            pltpu.VMEM((length, HEAD_WIDTH), jnp.float32),
            pltpu.VMEM((length, HEAD_WIDTH), jnp.float32),
        ],
        compiler_params=PARAMS,
        cost_estimate=pl.CostEstimate(flops=flops, bytes_accessed=6 << 20, transcendentals=0),
        name="student_backward",
    )(order, held, probs, out, grad)


def by_group(rows, groups):
    tokens, wide = rows.shape
    return jnp.transpose(rows.reshape(tokens, groups, wide // groups), (1, 0, 2))


def by_shared_head(rows, groups):
    heads = rows.shape[1] // HEAD_WIDTH
    return jnp.repeat(by_group(rows, heads), groups // heads, axis=0)


def shards(
    t_query,
    t_key,
    t_value,
    s_query,
    s_key,
    student_value,
    student_wo,
    projection,
    doc_ids,
    span_order,
):
    groups = lax.axis_size("seq")
    tokens = t_query.shape[1]
    length = tokens * groups
    halves = span_order.shape[1]
    t_local = t_query.shape[2] // HEAD_WIDTH // groups
    s_heads = s_query.shape[2] // HEAD_WIDTH
    s_local = s_heads // groups
    s_kv = s_key.shape[2] // HEAD_WIDTH
    order = span_order[0]
    places = jnp.arange(halves, dtype=jnp.int32)
    inverse = jnp.sum(
        jnp.where(order[None, :] == places[:, None], places[None, :], 0), axis=1, dtype=jnp.int32
    )
    col = doc_ids.reshape(length, 1)
    row = doc_ids.reshape(1, length)

    s_pack = jnp.concatenate(
        [
            by_group(s_query[0], groups),
            by_shared_head(s_key[0], groups),
            by_shared_head(student_value[0], groups),
        ],
        axis=2,
    )
    t_pack = jnp.concatenate(
        [
            by_group(t_query[0], groups),
            by_shared_head(t_key[0], groups),
            by_shared_head(t_value[0], groups),
        ],
        axis=2,
    )
    s_rows = lax.all_to_all(s_pack, "seq", split_axis=0, concat_axis=0, tiled=True)
    t_rows = lax.all_to_all(t_pack, "seq", split_axis=0, concat_axis=0, tiled=True)
    s_rows = s_rows.reshape(length, s_pack.shape[2])
    t_rows = t_rows.reshape(length, t_pack.shape[2])
    student_out, held, probs = student_attention(s_local, halves, inverse, s_rows, col, row)
    teacher_out = teacher_attention(t_local, halves, inverse, t_rows, col, row)

    width_all = student_wo.shape[1]
    own_diff = lax.psum_scatter(
        (
            jnp.dot(student_out, student_wo, preferred_element_type=jnp.float32)
            - jnp.dot(teacher_out, projection, preferred_element_type=jnp.float32)
        ).astype(jnp.bfloat16),
        "seq",
        scatter_dimension=0,
        tiled=True,
    )
    grad = lax.all_gather(own_diff, "seq", axis=0, tiled=True)
    grad32 = grad.astype(jnp.float32)
    seq_loss = (jnp.sum(grad32 * grad32) / (length * width_all)).reshape(1)
    d_weight = lax.dot_general(student_out, grad, TN, preferred_element_type=jnp.float32)
    weight_share = lax.psum_scatter(
        d_weight.astype(jnp.bfloat16), "rep", scatter_dimension=1, tiled=True
    ).astype(jnp.float32)
    d_attn = lax.dot_general(grad, student_wo, NT, preferred_element_type=jnp.float32).astype(
        jnp.bfloat16
    )
    back = student_backward(s_local, halves, order, held, probs, student_out, d_attn)
    back = lax.all_to_all(
        back.reshape(groups, tokens, back.shape[1]), "seq", split_axis=0, concat_axis=0, tiled=True
    )
    at = s_local * HEAD_WIDTH
    d_query = jnp.transpose(back[:, :, :at], (1, 0, 2)).reshape(1, tokens, s_heads * HEAD_WIDTH)

    def merge(parts):
        summed = parts.reshape(s_kv, groups // s_kv, tokens, HEAD_WIDTH).astype(jnp.float32)
        summed = summed.sum(axis=1).astype(jnp.bfloat16)
        return jnp.transpose(summed, (1, 0, 2)).reshape(1, tokens, s_kv * HEAD_WIDTH)

    return (
        seq_loss,
        weight_share,
        d_query,
        merge(back[:, :, at : at + HEAD_WIDTH]),
        merge(back[:, :, at + HEAD_WIDTH :]),
    )


def solution(mesh):
    in_specs = (
        P("rep", "seq", None),
        P("rep", "seq", None),
        P("rep", "seq", None),
        P("rep", "seq", None),
        P("rep", "seq", None),
        P("rep", "seq", None),
        P("seq", None),
        P("seq", None),
        P("rep", None),
        P("rep", None),
    )
    out_specs = (
        P("rep"),
        P("seq", "rep"),
        P("rep", "seq", None),
        P("rep", "seq", None),
        P("rep", "seq", None),
    )
    return jax.shard_map(shards, mesh=mesh, in_specs=in_specs, out_specs=out_specs, check_vma=False)
```

time: 484 us -> 312 us (0.64); the launches traced: 476 us -> 310 us
  waiting for transfers between devices: 285 us -> 226 us
  local copies, waits for them, and re-layouts: 46.9 us -> 13.5 us
  matrix products: 47 us -> 14 us
  other arithmetic: 30 us -> 10.4 us
  blocking collectives: 18.8 us -> 0 us
  Pallas kernels: 0 us -> 12.8 us
  starting transfers between devices: 29.7 us -> 18 us
    all_gather x5 -> x1, waiting for transfers between devices: 183 us -> 72.9 us  [shards(): grad = lax.all_gather(own_diff, 'seq', axis=0, tiled=True)]
    all_to_all x5 -> x3, waiting for transfers between devices: 11.4 us -> 59.7 us  [the longest x1 26.8 us: shards(): lax.all_to_all(t_pack, 'seq', split_axis=0, concat_axis=0, tiled=True)]
    dot_general x16 -> x2, matrix products: 32 us -> 8.39 us  [the longest x1 4.46 us: shards(): lax.dot_general(student_out, grad, TN, preferred_element_type=jnp.float32)]
    psum x1 -> x0, blocking collectives: 18.8 us -> none  [shards(): squares = lax.psum(jnp.sum(own_diff * own_diff), 'seq')]
    pallas_call x0 -> x3, Pallas kernels: none -> 12.8 us  [the longest x1 4.48 us: teacher_attention(): pl.pallas_call(functools.partial(teacher_kernel, heads, halves), out_shap...]
    all_to_all x5 -> x3, starting transfers between devices: 29.2 us -> 17.8 us  [the longest x1 6.35 us: shards(): lax.all_to_all(t_pack, 'seq', split_axis=0, concat_axis=0, tiled=True)]
    dynamic_update_slice x2 -> x0, other arithmetic: 8.3 us -> none  [head_attention(): return lax.map(one_block, block_ids)]
    sub x2 -> x0, matrix products: 8.15 us -> none  [one_block(): weights = jnp.where(allowed, jnp.exp(scores - maximum), 0.0)]
  transfers between devices with their start and end apart: 12 -> 6, of which waited for: 9 -> 6; matrix products, arithmetic and copies ran while one was open for 18% -> 6% of each run, Pallas kernels for 0% -> 1%
where the time goes in v1:
time: 312 us; the launch traced here: 310 us
  waiting for transfers between devices  226 us (72%)
  starting transfers between devices  18 us (6%)
  between operations  15.8 us (5%)
  matrix products  14 us (4%)
  local copies, waits for them, and re-layouts  13.5 us (4%)
  Pallas kernels  12.8 us (4%)
  other arithmetic  10.4 us (3%)
    reduce_scatter x1, waiting for transfers between devices, shards(): lax.psum_scatter((jnp.dot(student_out, student_wo, preferred_element_type...  89.8 us
    all_gather x1, waiting for transfers between devices, shards(): grad = lax.all_gather(own_diff, 'seq', axis=0, tiled=True)  72.9 us
    all_to_all x1, waiting for transfers between devices, shards(): lax.all_to_all(t_pack, 'seq', split_axis=0, concat_axis=0, tiled=True)  26.8 us
    all_to_all x1, waiting for transfers between devices, shards(): lax.all_to_all(s_pack, 'seq', split_axis=0, concat_axis=0, tiled=True)  19.7 us
    all_to_all x1, waiting for transfers between devices, shards(): lax.all_to_all(back.reshape(groups, tokens, back.shape[1]), 'seq', split_...  13.1 us
    unnamed x28, local copies, waits for them, and re-layouts  7.76 us
    all_to_all x1, starting transfers between devices, shards(): lax.all_to_all(t_pack, 'seq', split_axis=0, concat_axis=0, tiled=True)  6.35 us
  transfers between devices with their start and end apart: 6, of which 6 were waited for; matrix products, arithmetic and copies ran while one was open for 6% of the time, Pallas kernels for 1%

profile of v1, /device:TPU:11, one launch (start us, length us, event | category | flops | bytes accessed | tf_op | source)
XLA Modules:
  0.0 310.0 jit_solution(4080462107755138575)
XLA Ops:
  7.2 0.0 copy-start
  7.2 1.1 reshape_squeeze.19
  8.3 0.9 reshape_squeeze.20
  9.3 1.2 copy.66
  10.4 0.0 copy-start.10
  10.4 0.0 copy-start.11
  10.5 0.1 copy.71
  10.7 1.1 pad_maximum_fusion.1
  11.7 5.7 %all-to-all-start = ((bf16[8,128,512]{2,1,0:T(8,128)(2,1)}), bf16[8,128,512]{2,1,0:T(8,128)(2,1)S(1)}, u32[]{:S(2)}, u32[]{:S(2)}) async-start(bf16[8,128,512]{2,1,0:T(8,128)(2,1)} %pad_maximum_fusion.1), calls=%async_computation | async-start | bytes 2097152 | tf_op jit(solution)/shard_map/all_to_all | solution.py:250
  17.5 1.6 copy.67
  19.2 0.3 copy.70
  19.6 0.0 copy-start.7
  19.6 0.0 copy-start.8
  19.6 1.3 pad_maximum_fusion
  20.9 19.7 %all-to-all-done = bf16[8,128,512]{2,1,0:T(8,128)(2,1)S(1)} async-done(((bf16[8,128,512]{2,1,0:T(8,128)(2,1)}), bf16[8,128,512]{2,1,0:T(8,128)(2,1)S(1)}, u32[]{:S(2)}, u32[]{:S(2)}) %all-to-all-start) | async-done | bytes 1048608 | tf_op jit(solution)/shard_map/all_to_all | solution.py:250
  40.6 6.3 %all-to-all-start.1 = ((bf16[8,128,768]{2,1,0:T(8,128)(2,1)}), bf16[8,128,768]{2,1,0:T(8,128)(2,1)}, u32[]{:S(2)}, u32[]{:S(2)}) async-start(bf16[8,128,768]{2,1,0:T(8,128)(2,1)} %pad_maximum_fusion), calls=%async_computation.1 | async-start | bytes 3145728 | tf_op jit(solution)/shard_map/all_to_all | solution.py:251
  47.0 0.2 copy.56.col_ref
  47.2 0.1 select_reduce_fusion.inverse_ref
  47.3 1.2 copy-done.2
  48.5 3.9 %student_attention.1 = (bf16[1024,256]{1,0:T(8,128)(2,1)S(1)}, bf16[1024,512]{1,0:T(8,128)(2,1)S(1)}, bf16[8,256,384]{2,1,0:T(8,128)(2,1)S(1)}) custom-call(s32[16]{0:T(128)S(1)} %select_reduce_fusion.inverse_ref, bf16[1024,512]{1,0:T(8,128)(2,1)S(1)} %bitcast.44, s32[1024,1]{1,0:T(8,128)S(1)} %copy.56.col_ref, s32[1,1024]{1,0:T(1,128)S(1)} %copy-done.7), custom_call_target="tpu_custom_call" | custom-call | flops 402653184 | bytes 6291456 | tf_op jit(solution)/shard_map/student_attention/pallas_call | solution.py:162
  52.4 1.2 copy-done.3
  53.6 1.0 copy-done.5
  54.6 26.8 %all-to-all-done.1 = bf16[8,128,768]{2,1,0:T(8,128)(2,1)} async-done(((bf16[8,128,768]{2,1,0:T(8,128)(2,1)}), bf16[8,128,768]{2,1,0:T(8,128)(2,1)}, u32[]{:S(2)}, u32[]{:S(2)}) %all-to-all-start.1) | async-done | bytes 1572896 | tf_op jit(solution)/shard_map/all_to_all | solution.py:251
  81.4 4.5 %teacher_attention.1 = bf16[1024,512]{1,0:T(8,128)(2,1)S(1)} custom-call(s32[16]{0:T(128)S(1)} %select_reduce_fusion.inverse_ref, bf16[1024,768]{1,0:T(8,128)(2,1)} %bitcast.13.pack_ref, s32[1024,1]{1,0:T(8,128)S(1)} %copy.56.col_ref, s32[1,1024]{1,0:T(1,128)S(1)} %copy-done.7), custom_call_target="tpu_custom_call" | custom-call | flops 805306368 | bytes 4194304 | tf_op jit(solution)/shard_map/teacher_attention/pallas_call | solution.py:147
  85.9 2.3 fusion
  88.3 3.2 %subtract_convert_fusion = bf16[1024,2048]{1,0:T(8,128)(2,1)} fusion(f32[1024,2048]{1,0:T(8,128)S(1)} %fusion, bf16[1024,256]{1,0:T(8,128)(2,1)S(1)} %get-tuple-element.8.so_ref, bf16[256,2048]{1,0:T(8,128)(2,1)S(1)} %copy-done.9), kind=kOutput, calls=%fused_computation.1 | convolution fusion | flops 1077936128 | bytes 14155776 | tf_op jit(solution)/shard_map/dot_general | solution.py:260
  91.5 0.0 reduce-scatter.3.cloned.1.call-update
  91.6 0.2 all-gather.2.cloned.1.call-start
  91.8 89.8 %reduce-scatter.3.cloned.1.call-done = bf16[128,2048]{1,0:T(8,128)(2,1)} async-done(((bf16[1024,2048]{1,0:T(8,128)(2,1)}), bf16[128,2048]{1,0:T(8,128)(2,1)}) %reduce-scatter.3.cloned.1.call-update) | async-done | bytes 524304 | tf_op jit(solution)/shard_map/reduce_scatter | solution.py:258
  181.6 0.0 all-gather.2.cloned.1.call-update
  181.6 72.9 %all-gather.2.cloned.1.call-done = bf16[1024,2048]{1,0:T(8,128)(2,1)} async-done(((bf16[128,2048]{1,0:T(8,128)(2,1)}), bf16[1024,2048]{1,0:T(8,128)(2,1)}) %all-gather.2.cloned.1.call-update) | async-done | bytes 4194320 | tf_op jit(solution)/shard_map/all_gather | solution.py:267
  254.5 3.9 %convolution_convert_fusion.1.grad_ref = bf16[1024,256]{1,0:T(8,128)(2,1)S(1)} fusion(bf16[1024,2048]{1,0:T(8,128)(2,1)} %all-gather.2.cloned.1.call-done, bf16[256,2048]{1,0:T(8,128)(2,1)} %param.16), kind=kOutput, calls=%fused_computation.4 | convolution fusion | flops 1074003968 | bytes 5767168 | tf_op jit(solution)/shard_map/dot_general | solution.py:274
  258.4 4.4 %student_backward.1 = bf16[1024,512]{1,0:T(8,128)(2,1)} custom-call(s32[16]{0:T(128)S(1)} %bitcast.47, bf16[1024,512]{1,0:T(8,128)(2,1)S(1)} %copy-done.6, bf16[8,256,384]{2,1,0:T(8,128)(2,1)S(1)} %copy-done.4, bf16[1024,256]{1,0:T(8,128)(2,1)S(1)} %get-tuple-element.8.so_ref, bf16[1024,256]{1,0:T(8,128)(2,1)S(1)} %convolution_convert_fusion.1.grad_ref), custom_call_target="tpu_custom_call" | custom-call | flops 1006632960 | bytes 6291456 | tf_op jit(solution)/shard_map/student_backward/pallas_call | solution.py:180
  262.9 5.8 %all-to-all-start.2 = ((bf16[8,128,512]{2,1,0:T(8,128)(2,1)}), bf16[8,128,512]{2,1,0:T(8,128)(2,1)}, u32[]{:S(2)}, u32[]{:S(2)}) async-start(bf16[8,128,512]{2,1,0:T(8,128)(2,1)} %bitcast.15), calls=%async_computation.4 | async-start | bytes 2097152 | tf_op jit(solution)/shard_map/all_to_all | solution.py:278
  268.7 4.5 %convolution_convert_fusion = bf16[256,2048]{1,0:T(8,128)(2,1)} fusion(bf16[1024,256]{1,0:T(8,128)(2,1)S(1)} %get-tuple-element.8.so_ref, bf16[1024,2048]{1,0:T(8,128)(2,1)} %all-gather.2.cloned.1.call-done), kind=kOutput, calls=%fused_computation.2 | convolution fusion | flops 1074266112 | bytes 5767168 | tf_op jit(solution)/shard_map/dot_general | solution.py:270
  273.1 0.0 reduce-scatter.5.cloned.1.call-update
  273.2 5.0 %multiply_reduce_fusion = f32[]{:T(128)} fusion(bf16[1024,2048]{1,0:T(8,128)(2,1)} %all-gather.2.cloned.1.call-done), kind=kLoop, calls=%fused_computation | loop fusion | flops 6291455 | bytes 4194308 | tf_op jit(solution)/shard_map/reduce_sum | solution.py:269
  278.8 13.1 %all-to-all-done.2 = bf16[8,128,512]{2,1,0:T(8,128)(2,1)} async-done(((bf16[8,128,512]{2,1,0:T(8,128)(2,1)}), bf16[8,128,512]{2,1,0:T(8,128)(2,1)}, u32[]{:S(2)}, u32[]{:S(2)}) %all-to-all-start.2) | async-done | bytes 1048608 | tf_op jit(solution)/shard_map/all_to_all | solution.py:278
  291.9 1.2 slice_bitcast_fusion
  293.0 0.3 copy.61
  293.3 1.0 reshape.61
  294.4 1.1 bitcast_reduce_fusion
  295.5 0.1 copy.63
  295.6 0.8 copy.65
  296.4 0.1 copy.62
  296.5 0.8 copy.64
  297.3 3.3 %reduce-scatter.5.cloned.1.call-done = bf16[256,512]{1,0:T(8,128)(2,1)} async-done(((bf16[256,2048]{1,0:T(8,128)(2,1)}), bf16[256,512]{1,0:T(8,128)(2,1)}) %reduce-scatter.5.cloned.1.call-update) | async-done | bytes 262160 | tf_op jit(solution)/shard_map/reduce_scatter | solution.py:271
  300.6 1.8 convert_element_type.22
  (28 shorter events, 0.3 us)
Async XLA Ops:
  7.2 78.7 %copy-start = (bf16[512,2048]{1,0:T(8,128)(2,1)S(1)}, bf16[512,2048]{1,0:T(8,128)(2,1)}, u32[]{:S(2)}) copy-start(bf16[512,2048]{1,0:T(8,128)(2,1)} %param.17) | copy-start | bytes 6291460
  10.4 7.0 %copy-start.10 = (bf16[1,128,512]{2,1,0:T(8,128)(2,1)S(1)}, bf16[1,128,512]{2,1,0:T(8,128)(2,1)}, u32[]{:S(2)}) copy-start(bf16[1,128,512]{2,1,0:T(8,128)(2,1)} %param.11) | copy-start | bytes 393220
  10.4 7.0 %copy-start.11 = (bf16[1,128,512]{2,1,0:T(8,128)(2,1)S(1)}, bf16[1,128,512]{2,1,0:T(8,128)(2,1)}, u32[]{:S(2)}) copy-start(bf16[1,128,512]{2,1,0:T(8,128)(2,1)} %param.12) | copy-start | bytes 393220
  11.7 28.9 %all-to-all-start = ((bf16[8,128,512]{2,1,0:T(8,128)(2,1)}), bf16[8,128,512]{2,1,0:T(8,128)(2,1)S(1)}, u32[]{:S(2)}, u32[]{:S(2)}) async-start(bf16[8,128,512]{2,1,0:T(8,128)(2,1)} %pad_maximum_fusion.1), calls=%async_computation | async-start | bytes 2097152 | tf_op jit(solution)/shard_map/all_to_all | solution.py:250
  19.6 27.4 %copy-start.7 = (s32[1,1024]{1,0:T(1,128)S(1)}, s32[1,1024]{1,0:T(1,128)}, u32[]{:S(2)}) copy-start(s32[1,1024]{1,0:T(1,128)} %row_ref.3) | copy-start | bytes 12292
  19.6 27.6 %copy-start.8 = (s32[1,16]{1,0:T(1,128)S(1)}, s32[1,16]{1,0:T(1,128)}, u32[]{:S(2)}) copy-start(s32[1,16]{1,0:T(1,128)} %param.19) | copy-start | bytes 196
  40.6 6.4 %copy-start.1 = (bf16[8,128,512]{2,1,0:T(8,128)(2,1)}, bf16[8,128,512]{2,1,0:T(8,128)(2,1)S(1)}, u32[]{:S(2)}) copy-start(bf16[8,128,512]{2,1,0:T(8,128)(2,1)S(1)} %all-to-all-done) | copy-start | bytes 3145732
  40.6 40.8 %all-to-all-start.1 = ((bf16[8,128,768]{2,1,0:T(8,128)(2,1)}), bf16[8,128,768]{2,1,0:T(8,128)(2,1)}, u32[]{:S(2)}, u32[]{:S(2)}) async-start(bf16[8,128,768]{2,1,0:T(8,128)(2,1)} %pad_maximum_fusion), calls=%async_computation.1 | async-start | bytes 3145728 | tf_op jit(solution)/shard_map/all_to_all | solution.py:251
  46.9 134.6 %reduce-scatter.3.cloned.1.call-start = ((), (), s32[]{:S(2)}) async-start(), calls=%async_computation.5 | async-start | bytes 4718592 | tf_op jit(solution)/shard_map/reduce_scatter | solution.py:258
  47.3 1.2 copy-start.2
  52.4 1.2 copy-start.3
  53.6 1.0 copy-start.5
  85.9 2.4 copy-start.9
  91.6 162.9 %all-gather.2.cloned.1.call-start = ((), (), s32[]{:S(2)}) async-start(), calls=%async_computation.6 | async-start | bytes 4718592 | tf_op jit(solution)/shard_map/all_gather | solution.py:267
  254.5 3.9 %copy-start.4 = (bf16[8,256,384]{2,1,0:T(8,128)(2,1)S(1)}, bf16[8,256,384]{2,1,0:T(8,128)(2,1)}, u32[]{:S(2)}) copy-start(bf16[8,256,384]{2,1,0:T(8,128)(2,1)} %copy-done.3) | copy-start | bytes 4718596
  254.5 3.9 %copy-start.6 = (bf16[1024,512]{1,0:T(8,128)(2,1)S(1)}, bf16[1024,512]{1,0:T(8,128)(2,1)}, u32[]{:S(2)}) copy-start(bf16[1024,512]{1,0:T(8,128)(2,1)} %copy-done.5) | copy-start | bytes 3145732
  262.9 29.0 %all-to-all-start.2 = ((bf16[8,128,512]{2,1,0:T(8,128)(2,1)}), bf16[8,128,512]{2,1,0:T(8,128)(2,1)}, u32[]{:S(2)}, u32[]{:S(2)}) async-start(bf16[8,128,512]{2,1,0:T(8,128)(2,1)} %bitcast.15), calls=%async_computation.4 | async-start | bytes 2097152 | tf_op jit(solution)/shard_map/all_to_all | solution.py:278
  268.7 31.9 %reduce-scatter.5.cloned.1.call-start = ((), (), s32[]{:S(2)}) async-start(), calls=%async_computation.7 | async-start | bytes 1310720 | tf_op jit(solution)/shard_map/reduce_scatter | solution.py:271
Sparse Core Ops, SparseCore 0:
  91.7 89.8 reduce-scatter.2
  183.9 70.4 all-gather.1
  273.3 27.2 reduce-scatter.4

commit v2 on v1

--- a/solution.py
+++ b/solution.py
@@ -10,6 +10,7 @@
 
 HEAD_WIDTH = 128
 ROWS = 128
+CHUNKS = 8
 MASKED = -1e30
 VMEM_LIMIT = 48 * 1024 * 1024
 NT = (((1,), (1,)), ((), ()))
@@ -191,6 +192,174 @@
         cost_estimate=pl.CostEstimate(flops=flops, bytes_accessed=6 << 20, transcendentals=0),
         name="student_backward",
     )(order, held, probs, out, grad)
+
+
+def exchange_kernel(
+    chain, chunks, so_ref, to_ref, wo_ref, pj_ref, attn_ref, dw_ref, loss_ref,
+    pair_out, pair_in, kept, far_out, far_in, grad, total,
+    ps, pr, zs, zr, gs, gr, fs, fr,
+):
+    me = lax.axis_index("seq")
+    mine, side = me // 2, me % 2
+    other = 1 - side
+    tokens = so_ref.shape[2]
+    width = grad.shape[3]
+    length = chain * 2 * tokens
+    partner = {"seq": mine * 2 + other}
+    peers = [lax.rem(mine + d, chain) for d in range(1, chain)]
+
+    barrier = pltpu.get_barrier_semaphore()
+    pl.semaphore_signal(barrier, inc=1, device_id=partner, device_id_type=pl.DeviceIdType.MESH)
+    for peer in peers:
+        pl.semaphore_signal(
+            barrier, inc=1, device_id={"seq": peer * 2 + side}, device_id_type=pl.DeviceIdType.MESH
+        )
+    pl.semaphore_wait(barrier, chain)
+
+    def copy(source, target, send, receive, device):
+        return pltpu.make_async_remote_copy(
+            src_ref=source, dst_ref=target, send_sem=send, recv_sem=receive,
+            device_id=device, device_id_type=pl.DeviceIdType.MESH,
+        )
+
+    def pair_copy(c, t):
+        return copy(pair_out.at[c, t], pair_in.at[c, t], ps.at[c, t], pr.at[c, t], partner)
+
+    def far_copy(c, t):
+        return copy(
+            far_out.at[c, t], far_in.at[c, mine], zs.at[c, t], zr.at[c, mine], {"seq": t * 2 + side}
+        )
+
+    def far_arrival(c, t):
+        return copy(
+            far_out.at[c, t], far_in.at[c, t], zs.at[c, t], zr.at[c, t], {"seq": t * 2 + side}
+        )
+
+    def grad_copy(c, t):
+        return copy(
+            grad.at[c, me], grad.at[c, me], gs.at[c, t], gr.at[c, mine], {"seq": t * 2 + side}
+        )
+
+    def grad_arrival(c, t):
+        block = grad.at[c, t * 2 + side]
+        return copy(block, block, gs.at[c, t], gr.at[c, t], {"seq": t * 2 + side})
+
+    def side_copy(c, t):
+        block = grad.at[c, t * 2 + side]
+        return copy(block, block, fs.at[c, t], fr.at[c, t], partner)
+
+    def side_arrival(c, t):
+        block = grad.at[c, t * 2 + other]
+        return copy(block, block, fs.at[c, t], fr.at[c, t], partner)
+
+    def partial(c, which):
+        columns = slice(c * width, (c + 1) * width)
+        rows = chain * tokens
+        term = jnp.dot(
+            so_ref[:, which].reshape(rows, so_ref.shape[3]), wo_ref[:, columns],
+            preferred_element_type=jnp.float32,
+        ) - jnp.dot(
+            to_ref[:, which].reshape(rows, to_ref.shape[3]), pj_ref[:, columns],
+            preferred_element_type=jnp.float32,
+        )
+        return term.astype(jnp.bfloat16).reshape(chain, tokens, width)
+
+    def first_stage(c):
+        pair_out[c] = partial(c, other)
+        for t in range(chain):
+            pair_copy(c, t).start()
+        kept[c] = partial(c, side)
+
+    def second_stage(c):
+        for t in range(chain):
+            pair_copy(c, t).wait_recv()
+        far_out[c] = (kept[c].astype(jnp.float32) + pair_in[c].astype(jnp.float32)).astype(
+            jnp.bfloat16
+        )
+        for peer in peers:
+            far_copy(c, peer).start()
+
+    def third_stage(c):
+        summed = kept[c, mine].astype(jnp.float32) + pair_in[c, mine].astype(jnp.float32)
+        for peer in peers:
+            far_arrival(c, peer).wait_recv()
+            summed = summed + far_in[c, peer].astype(jnp.float32)
+        grad[c, me] = summed.astype(jnp.bfloat16)
+        side_copy(c, mine).start()
+        for peer in peers:
+            grad_copy(c, peer).start()
+
+    def fourth_stage(c):
+        for peer in peers:
+            grad_arrival(c, peer).wait_recv()
+            side_copy(c, peer).start()
+
+    def fifth_stage(c):
+        for t in range(chain):
+            side_arrival(c, t).wait_recv()
+        columns = slice(c * width, (c + 1) * width)
+        block = grad[c].reshape(length, width)
+        wide = block.astype(jnp.float32)
+        squares = jnp.sum(wide * wide, axis=0, keepdims=True)
+        d_attn = lax.dot_general(block, wo_ref[:, columns], NT, preferred_element_type=jnp.float32)
+        if c == 0:
+            loss_ref[...] = squares
+            total[...] = d_attn
+        else:
+            loss_ref[...] += squares
+            total[...] += d_attn
+        dw_ref[:, columns] = lax.dot_general(
+            so_ref[...].reshape(length, so_ref.shape[3]), block, TN,
+            preferred_element_type=jnp.float32,
+        ).astype(jnp.bfloat16)
+
+    stages = ((first_stage, 0), (second_stage, 2), (third_stage, 3), (fourth_stage, 4), (fifth_stage, 5))
+    for step in range(chunks + 5):
+        for stage, lag in stages:
+            if 0 <= step - lag < chunks:
+                stage(step - lag)
+    attn_ref[...] = total[...].astype(jnp.bfloat16)
+    for c in range(chunks):
+        for t in range(chain):
+            pair_copy(c, t).wait_send()
+            side_copy(c, t).wait_send()
+        for peer in peers:
+            far_copy(c, peer).wait_send()
+            grad_copy(c, peer).wait_send()
+
+
+def exchange(groups, chunks, student_out, teacher_out, student_wo, projection):
+    length, ws = student_out.shape
+    wt = teacher_out.shape[1]
+    chain, tokens = groups // 2, length // groups
+    columns = student_wo.shape[1]
+    width = columns // chunks
+    block = (chunks, chain, tokens, width)
+    sems = pltpu.SemaphoreType.DMA((chunks, chain))
+    return pl.pallas_call(
+        functools.partial(exchange_kernel, chain, chunks),
+        out_shape=(
+            shape((length, ws)), shape((ws, columns)), shape((1, width), jnp.float32),
+        ),
+        in_specs=[VMEM] * 4,
+        out_specs=(VMEM, VMEM, VMEM),
+        scratch_shapes=[pltpu.VMEM(block, jnp.bfloat16)] * 5
+        + [
+            pltpu.VMEM((chunks, groups, tokens, width), jnp.bfloat16),
+            pltpu.VMEM((length, ws), jnp.float32),
+        ]
+        + [sems] * 8,
+        compiler_params=pltpu.CompilerParams(
+            collective_id=0, has_side_effects=True, vmem_limit_bytes=VMEM_LIMIT
+        ),
+        cost_estimate=pl.CostEstimate(
+            flops=2 * length * columns * (3 * ws + wt), bytes_accessed=8 << 20, transcendentals=0
+        ),
+        name="exchange",
+    )(
+        student_out.reshape(chain, 2, tokens, ws), teacher_out.reshape(chain, 2, tokens, wt),
+        student_wo, projection,
+    )
 
 
 def by_group(rows, groups):
@@ -255,25 +424,13 @@
     teacher_out = teacher_attention(t_local, halves, inverse, t_rows, col, row)
 
     width_all = student_wo.shape[1]
-    own_diff = lax.psum_scatter(
-        (
-            jnp.dot(student_out, student_wo, preferred_element_type=jnp.float32)
-            - jnp.dot(teacher_out, projection, preferred_element_type=jnp.float32)
-        ).astype(jnp.bfloat16),
-        "seq",
-        scatter_dimension=0,
-        tiled=True,
-    )
-    grad = lax.all_gather(own_diff, "seq", axis=0, tiled=True)
-    grad32 = grad.astype(jnp.float32)
-    seq_loss = (jnp.sum(grad32 * grad32) / (length * width_all)).reshape(1)
-    d_weight = lax.dot_general(student_out, grad, TN, preferred_element_type=jnp.float32)
+    d_attn, d_weight, squares = exchange(
+        groups, CHUNKS, student_out, teacher_out, student_wo, projection
+    )
+    seq_loss = (jnp.sum(squares) / (length * width_all)).reshape(1)
     weight_share = lax.psum_scatter(
-        d_weight.astype(jnp.bfloat16), "rep", scatter_dimension=1, tiled=True
+        d_weight, "rep", scatter_dimension=1, tiled=True
     ).astype(jnp.float32)
-    d_attn = lax.dot_general(grad, student_wo, NT, preferred_element_type=jnp.float32).astype(
-        jnp.bfloat16
-    )
     back = student_backward(s_local, halves, order, held, probs, student_out, d_attn)
     back = lax.all_to_all(
         back.reshape(groups, tokens, back.shape[1]), "seq", split_axis=0, concat_axis=0, tiled=True

time: 312 us -> 250 us (0.80)
  waiting for transfers between devices: 226 us -> 75.4 us
  Pallas kernels: 12.8 us -> 124 us
  matrix products: 14 us -> 0 us
  other arithmetic: 10.4 us -> 4.95 us
    pallas_call x0 -> x1, Pallas kernels: none -> 112 us  [exchange(): pl.pallas_call(functools.partial(exchange_kernel, chain, chunks), out_sha...]
    reduce_scatter x2 -> x1, waiting for transfers between devices: 93.1 us -> 5.65 us  [shards(): lax.psum_scatter(d_weight, 'rep', scatter_dimension=1, tiled=True)]
    all_gather x1 -> x0, waiting for transfers between devices: 72.9 us -> none  [shards(): grad = lax.all_gather(own_diff, 'seq', axis=0, tiled=True)]
    dot_general x4 -> x0, matrix products: 14 us -> none  [the longest x1 4.46 us: shards(): lax.dot_general(student_out, grad, TN, preferred_element_type=jnp.float32)]
    all_to_all x1, waiting for transfers between devices: 13.1 us -> 20.8 us  [shards(): lax.all_to_all(back.reshape(groups, tokens, back.shape[1]), 'seq', split_...]
    reduce_sum x1, other arithmetic: 4.95 us -> 0.6 us  [shards(): seq_loss = (jnp.sum(squares) / (length * width_all)).reshape(1)]
  transfers between devices with their start and end apart: 6 -> 4, of which waited for: 6 -> 4; matrix products, arithmetic and copies ran while one was open for 6% -> 3% of each run, Pallas kernels for 1% -> 2%
where the time goes in v2:
time: 250 us; the launch traced here: 248 us
  Pallas kernels  124 us (50%)
  waiting for transfers between devices  75.4 us (30%)
  starting transfers between devices  17.4 us (7%)
  between operations  16.1 us (6%)
  local copies, waits for them, and re-layouts  10.5 us (4%)
  other arithmetic  4.95 us (2%)
    pallas_call x1, Pallas kernels, exchange(): pl.pallas_call(functools.partial(exchange_kernel, chain, chunks), out_sha...  112 us
    all_to_all x1, waiting for transfers between devices, shards(): lax.all_to_all(t_pack, 'seq', split_axis=0, concat_axis=0, tiled=True)  27.3 us
    all_to_all x1, waiting for transfers between devices, shards(): lax.all_to_all(s_pack, 'seq', split_axis=0, concat_axis=0, tiled=True)  20.9 us
    all_to_all x1, waiting for transfers between devices, shards(): lax.all_to_all(back.reshape(groups, tokens, back.shape[1]), 'seq', split_...  20.8 us
    all_to_all x1, starting transfers between devices, shards(): lax.all_to_all(t_pack, 'seq', split_axis=0, concat_axis=0, tiled=True)  6.35 us
    unnamed x28, local copies, waits for them, and re-layouts  6.06 us
    all_to_all x1, starting transfers between devices, shards(): lax.all_to_all(s_pack, 'seq', split_axis=0, concat_axis=0, tiled=True)  5.79 us
    reduce_scatter x1, waiting for transfers between devices, shards(): lax.psum_scatter(d_weight, 'rep', scatter_dimension=1, tiled=True)  5.65 us
  transfers between devices with their start and end apart: 4, of which 4 were waited for; matrix products, arithmetic and copies ran while one was open for 3% of the time, Pallas kernels for 2%

profile of v2, /device:TPU:11, one launch (start us, length us, event | category | flops | bytes accessed | tf_op | source)
XLA Modules:
  0.0 248.1 jit_solution(6294666397713112000)
XLA Ops:
  7.2 0.9 reshape_squeeze.19
  8.1 0.9 reshape_squeeze.20
  9.1 1.2 copy.66
  10.3 0.1 copy.71
  10.5 0.0 copy-start.10
  10.5 0.0 copy-start.11
  10.5 1.1 pad_maximum_fusion.1
  11.6 5.8 %all-to-all-start = ((bf16[8,128,512]{2,1,0:T(8,128)(2,1)}), bf16[8,128,512]{2,1,0:T(8,128)(2,1)S(1)}, u32[]{:S(2)}, u32[]{:S(2)}) async-start(bf16[8,128,512]{2,1,0:T(8,128)(2,1)} %pad_maximum_fusion.1), calls=%async_computation | async-start | bytes 2097152 | tf_op jit(solution)/shard_map/all_to_all | solution.py:419
  17.4 0.0 copy-done.10
  17.4 0.0 copy-done.11
  17.5 0.0 copy-done.9
  17.5 0.4 copy.67
  17.9 0.3 copy.70
  18.3 1.3 pad_maximum_fusion
  19.6 20.9 %all-to-all-done = bf16[8,128,512]{2,1,0:T(8,128)(2,1)S(1)} async-done(((bf16[8,128,512]{2,1,0:T(8,128)(2,1)}), bf16[8,128,512]{2,1,0:T(8,128)(2,1)S(1)}, u32[]{:S(2)}, u32[]{:S(2)}) %all-to-all-start) | async-done | bytes 1048608 | tf_op jit(solution)/shard_map/all_to_all | solution.py:419
  40.6 6.3 %all-to-all-start.1 = ((bf16[8,128,768]{2,1,0:T(8,128)(2,1)}), bf16[8,128,768]{2,1,0:T(8,128)(2,1)S(1)}, u32[]{:S(2)}, u32[]{:S(2)}) async-start(bf16[8,128,768]{2,1,0:T(8,128)(2,1)} %pad_maximum_fusion), calls=%async_computation.1 | async-start | bytes 3145728 | tf_op jit(solution)/shard_map/all_to_all | solution.py:420
  46.9 0.0 copy-done.6
  46.9 0.2 copy.56.col_ref
  47.1 0.0 copy-done.7
  47.1 0.1 select_reduce_fusion.inverse_ref
  47.3 3.9 %student_attention.1 = (bf16[1024,256]{1,0:T(8,128)(2,1)S(1)}, bf16[1024,512]{1,0:T(8,128)(2,1)S(1)}, bf16[8,256,384]{2,1,0:T(8,128)(2,1)S(1)}) custom-call(s32[16]{0:T(128)S(1)} %select_reduce_fusion.inverse_ref, bf16[1024,512]{1,0:T(8,128)(2,1)S(1)} %bitcast.39, s32[1024,1]{1,0:T(8,128)S(1)} %copy.56.col_ref, s32[1,1024]{1,0:T(1,128)S(1)} %copy-done.6), custom_call_target="tpu_custom_call" | custom-call | flops 402653184 | bytes 6291456 | tf_op jit(solution)/shard_map/student_attention/pallas_call | solution.py:163
  51.1 0.0 copy-start
  51.1 1.1 copy-done
  52.3 1.0 copy-done.2
  53.3 0.8 copy-done.4
  54.1 27.3 %all-to-all-done.1 = bf16[8,128,768]{2,1,0:T(8,128)(2,1)S(1)} async-done(((bf16[8,128,768]{2,1,0:T(8,128)(2,1)}), bf16[8,128,768]{2,1,0:T(8,128)(2,1)S(1)}, u32[]{:S(2)}, u32[]{:S(2)}) %all-to-all-start.1) | async-done | bytes 1572896 | tf_op jit(solution)/shard_map/all_to_all | solution.py:420
  81.4 3.6 %teacher_attention.1 = bf16[1024,512]{1,0:T(8,128)(2,1)S(1)} custom-call(s32[16]{0:T(128)S(1)} %select_reduce_fusion.inverse_ref, bf16[1024,768]{1,0:T(8,128)(2,1)S(1)} %bitcast.38, s32[1024,1]{1,0:T(8,128)S(1)} %copy.56.col_ref, s32[1,1024]{1,0:T(1,128)S(1)} %copy-done.6), custom_call_target="tpu_custom_call" | custom-call | flops 805306368 | bytes 4194304 | tf_op jit(solution)/shard_map/teacher_attention/pallas_call | solution.py:148
  85.0 0.0 copy-done.8
  85.0 0.0 copy-done.5
  85.0 0.0 copy-start.1
  85.0 0.0 copy-start.3
  85.0 111.8 %exchange.1 = (bf16[1024,256]{1,0:T(8,128)(2,1)S(1)}, bf16[256,2048]{1,0:T(8,128)(2,1)}, f32[1,256]{1,0:T(1,128)S(1)}) custom-call(bf16[4,2,128,256]{3,2,1,0:T(8,128)(2,1)S(1)} %bitcast.41, bf16[4,2,128,512]{3,2,1,0:T(8,128)(2,1)S(1)} %bitcast.40, bf16[256,2048]{1,0:T(8,128)(2,1)S(1)} %copy-done.8, bf16[512,2048]{1,0:T(8,128)(2,1)} %pj_ref.1), custom_call_target="tpu_custom_call" | custom-call | flops 5368709120 | bytes 8388608 | tf_op jit(solution)/shard_map/exchange/pallas_call | solution.py:339
  196.8 0.0 copy-done.1
  196.8 0.0 copy-done.3
  196.8 4.5 %student_backward.1 = bf16[1024,512]{1,0:T(8,128)(2,1)} custom-call(s32[16]{0:T(128)S(1)} %bitcast.44, bf16[1024,512]{1,0:T(8,128)(2,1)S(1)} %copy-done.3, bf16[8,256,384]{2,1,0:T(8,128)(2,1)S(1)} %copy-done.1, bf16[1024,256]{1,0:T(8,128)(2,1)S(1)} %copy-done.5, bf16[1024,256]{1,0:T(8,128)(2,1)S(1)} %get-tuple-element.16.grad_ref), custom_call_target="tpu_custom_call" | custom-call | flops 1006632960 | bytes 6291456 | tf_op jit(solution)/shard_map/student_backward/pallas_call | solution.py:181
  201.3 5.3 %all-to-all-start.2 = ((bf16[8,128,512]{2,1,0:T(8,128)(2,1)}), bf16[8,128,512]{2,1,0:T(8,128)(2,1)S(1)}, u32[]{:S(2)}, u32[]{:S(2)}) async-start(bf16[8,128,512]{2,1,0:T(8,128)(2,1)} %bitcast.17), calls=%async_computation.3 | async-start | bytes 2097152 | tf_op jit(solution)/shard_map/all_to_all | solution.py:435
  206.6 0.7 reduce-scatter.2.cloned.1.call-update
  207.3 0.6 reduce_sum.43
  208.6 20.8 %all-to-all-done.2 = bf16[8,128,512]{2,1,0:T(8,128)(2,1)S(1)} async-done(((bf16[8,128,512]{2,1,0:T(8,128)(2,1)}), bf16[8,128,512]{2,1,0:T(8,128)(2,1)S(1)}, u32[]{:S(2)}, u32[]{:S(2)}) %all-to-all-start.2) | async-done | bytes 1048608 | tf_op jit(solution)/shard_map/all_to_all | solution.py:435
  229.4 0.3 copy.61
  229.7 1.0 reshape.69
  230.7 0.1 bitcast_reduce_fusion
  230.8 0.1 copy.63
  230.9 0.8 copy.65
  231.7 0.1 copy.62
  231.8 0.8 copy.64
  232.6 5.6 %reduce-scatter.2.cloned.1.call-done = bf16[256,512]{1,0:T(8,128)(2,1)} async-done(((bf16[256,2048]{1,0:T(8,128)(2,1)}), bf16[256,512]{1,0:T(8,128)(2,1)}) %reduce-scatter.2.cloned.1.call-update) | async-done | bytes 262160 | tf_op jit(solution)/shard_map/reduce_scatter | solution.py:431
  238.3 1.8 convert_element_type.2
  (19 shorter events, 0.3 us)
Async XLA Ops:
  10.5 6.9 %copy-start.10 = (bf16[1,128,512]{2,1,0:T(8,128)(2,1)S(1)}, bf16[1,128,512]{2,1,0:T(8,128)(2,1)}, u32[]{:S(2)}) copy-start(bf16[1,128,512]{2,1,0:T(8,128)(2,1)} %param.11) | copy-start | bytes 393220
  10.5 7.0 %copy-start.11 = (bf16[1,128,512]{2,1,0:T(8,128)(2,1)S(1)}, bf16[1,128,512]{2,1,0:T(8,128)(2,1)}, u32[]{:S(2)}) copy-start(bf16[1,128,512]{2,1,0:T(8,128)(2,1)} %param.12) | copy-start | bytes 393220
  11.6 5.9 %copy-start.9 = (bf16[1,128,4096]{2,1,0:T(8,128)(2,1)S(1)}, bf16[1,128,4096]{2,1,0:T(8,128)(2,1)}, u32[]{:S(2)}) copy-start(bf16[1,128,4096]{2,1,0:T(8,128)(2,1)} %param.10) | copy-start | bytes 3145732
  11.6 29.0 %all-to-all-start = ((bf16[8,128,512]{2,1,0:T(8,128)(2,1)}), bf16[8,128,512]{2,1,0:T(8,128)(2,1)S(1)}, u32[]{:S(2)}, u32[]{:S(2)}) async-start(bf16[8,128,512]{2,1,0:T(8,128)(2,1)} %pad_maximum_fusion.1), calls=%async_computation | async-start | bytes 2097152 | tf_op jit(solution)/shard_map/all_to_all | solution.py:419
  19.6 27.3 %copy-start.6 = (s32[1,1024]{1,0:T(1,128)S(1)}, s32[1,1024]{1,0:T(1,128)}, u32[]{:S(2)}) copy-start(s32[1,1024]{1,0:T(1,128)} %row_ref.3) | copy-start | bytes 12292
  19.6 27.5 %copy-start.7 = (s32[1,16]{1,0:T(1,128)S(1)}, s32[1,16]{1,0:T(1,128)}, u32[]{:S(2)}) copy-start(s32[1,16]{1,0:T(1,128)} %param.19) | copy-start | bytes 196
  40.6 40.8 %all-to-all-start.1 = ((bf16[8,128,768]{2,1,0:T(8,128)(2,1)}), bf16[8,128,768]{2,1,0:T(8,128)(2,1)S(1)}, u32[]{:S(2)}, u32[]{:S(2)}) async-start(bf16[8,128,768]{2,1,0:T(8,128)(2,1)} %pad_maximum_fusion), calls=%async_computation.1 | async-start | bytes 3145728 | tf_op jit(solution)/shard_map/all_to_all | solution.py:420
  51.1 1.1 copy-start
  52.3 1.0 copy-start.2
  53.3 0.8 copy-start.4
  54.1 30.9 %copy-start.8 = (bf16[256,2048]{1,0:T(8,128)(2,1)S(1)}, bf16[256,2048]{1,0:T(8,128)(2,1)}, u32[]{:S(2)}) copy-start(bf16[256,2048]{1,0:T(8,128)(2,1)} %wo_ref.1) | copy-start | bytes 3145732
  81.4 3.6 %copy-start.5 = (bf16[1024,256]{1,0:T(8,128)(2,1)S(1)}, bf16[1024,256]{1,0:T(8,128)(2,1)}, u32[]{:S(2)}) copy-start(bf16[1024,256]{1,0:T(8,128)(2,1)} %copy-done.4) | copy-start | bytes 1572868
  85.0 111.8 %copy-start.1 = (bf16[8,256,384]{2,1,0:T(8,128)(2,1)S(1)}, bf16[8,256,384]{2,1,0:T(8,128)(2,1)}, u32[]{:S(2)}) copy-start(bf16[8,256,384]{2,1,0:T(8,128)(2,1)} %copy-done) | copy-start | bytes 4718596
  85.0 111.8 %copy-start.3 = (bf16[1024,512]{1,0:T(8,128)(2,1)S(1)}, bf16[1024,512]{1,0:T(8,128)(2,1)}, u32[]{:S(2)}) copy-start(bf16[1024,512]{1,0:T(8,128)(2,1)} %copy-done.2) | copy-start | bytes 3145732
  201.3 28.0 %all-to-all-start.2 = ((bf16[8,128,512]{2,1,0:T(8,128)(2,1)}), bf16[8,128,512]{2,1,0:T(8,128)(2,1)S(1)}, u32[]{:S(2)}, u32[]{:S(2)}) async-start(bf16[8,128,512]{2,1,0:T(8,128)(2,1)} %bitcast.17), calls=%async_computation.3 | async-start | bytes 2097152 | tf_op jit(solution)/shard_map/all_to_all | solution.py:435
  206.6 31.7 %reduce-scatter.2.cloned.1.call-start = ((), (), s32[]{:S(2)}) async-start(), calls=%async_computation.4 | async-start | bytes 1310720 | tf_op jit(solution)/shard_map/reduce_scatter | solution.py:431
Sparse Core Ops, SparseCore 0:
  209.9 28.2 reduce-scatter.1

commit v3 on v2

--- a/solution.py
+++ b/solution.py
@@ -10,7 +10,8 @@
 
 HEAD_WIDTH = 128
 ROWS = 128
-CHUNKS = 8
+PICKED = 256
+CHUNKS = 16
 MASKED = -1e30
 VMEM_LIMIT = 48 * 1024 * 1024
 NT = (((1,), (1,)), ((), ()))
@@ -23,12 +24,6 @@
     for first in range(0, length, ROWS):
         out.append((first, max(0, first - reach), first + ROWS))
     return out
-
-
-def to_true_order(inverse_ref, source_ref, target_ref, halves, half):
-    for place in range(halves):
-        start = pl.multiple_of(inverse_ref[place] * half, half)
-        target_ref[place * half : (place + 1) * half, :] = source_ref[pl.ds(start, half), :]
 
 
 def block_weights(heads, queries, keys, doc_col, doc_row, first, low, high):
@@ -51,9 +46,8 @@
     )
 
 
-def teacher_kernel(heads, halves, inverse_ref, pack_ref, col_ref, row_ref, out_ref, held):
-    length = pack_ref.shape[0]
-    to_true_order(inverse_ref, pack_ref, held, halves, length // halves)
+def teacher_blocks(heads, held, col_ref, row_ref, out_ref):
+    length = held.shape[0]
     at = heads * HEAD_WIDTH
     for first, low, high in windows(length):
         queries = stacked(held, heads, first, first + ROWS)
@@ -71,9 +65,8 @@
             out_ref[first : first + ROWS, h * HEAD_WIDTH : (h + 1) * HEAD_WIDTH] = mixed[h]
 
 
-def student_kernel(heads, halves, inverse_ref, pack_ref, col_ref, row_ref, out_ref, held, prob_ref):
-    length = pack_ref.shape[0]
-    to_true_order(inverse_ref, pack_ref, held, halves, length // halves)
+def student_blocks(heads, held, col_ref, row_ref, out_ref, prob_ref):
+    length = held.shape[0]
     at = heads * HEAD_WIDTH
     for i, (first, low, high) in enumerate(windows(length)):
         queries = stacked(held, heads, first, first + ROWS)
@@ -93,11 +86,164 @@
             ]
 
 
-def back_kernel(heads, halves, order_ref, held_ref, prob_ref, so_ref, grad_ref, out_ref, done, dk, dv):
+def reordered(source_rows, source):
+    count, length = source_rows.shape[0], source.shape[0]
+    places = lax.broadcasted_iota(jnp.int32, (count, length), 1)
+    picks = jnp.where(source_rows == places, 1.0, 0.0).astype(jnp.bfloat16)
+    return jnp.dot(picks, source, preferred_element_type=jnp.float32).astype(jnp.bfloat16)
+
+
+MESH = pl.DeviceIdType.MESH
+
+
+def greet(seq_peers, rep_peers=()):
+    barrier = pltpu.get_barrier_semaphore()
+    for peer in seq_peers:
+        pl.semaphore_signal(barrier, inc=1, device_id={"seq": peer}, device_id_type=MESH)
+    for peer in rep_peers:
+        pl.semaphore_signal(barrier, inc=1, device_id={"rep": peer}, device_id_type=MESH)
+    pl.semaphore_wait(barrier, len(seq_peers) + len(rep_peers))
+
+
+def remote(source, target, send, receive, device):
+    return pltpu.make_async_remote_copy(
+        src_ref=source, dst_ref=target, send_sem=send, recv_sem=receive,
+        device_id=device, device_id_type=MESH,
+    )
+
+
+def forward_kernel(
+    groups, halves, inverse_ref, tq_ref, tk_ref, tv_ref, sq_ref, sk_ref, sv_ref, col_ref, row_ref,
+    so_ref, held_ref, prob_ref, to_ref,
+    sq_out, sq_in, tq_out, tq_in, kv_out, kv_in, t_held,
+    sqs, sqr, tqs, tqr, kvs, kvr, fs, fr,
+):
+    me = lax.axis_index("seq")
+    mine, side = me // 2, me % 2
+    partner = mine * 2 + 1 - side
+    chain, per = groups // 2, halves // groups
+    half = sq_out.shape[2]
+    ws, wt = sq_out.shape[3], tq_out.shape[3]
+    kv_heads = kv_out.shape[0]
+    share = groups // kv_heads
+    everyone = [lax.rem(me + d, groups) for d in range(1, groups)]
+    peers = [lax.rem(mine + d, chain) for d in range(1, chain)]
+    greet(everyone)
+
+    for j in range(kv_heads):
+        columns = slice(j * HEAD_WIDTH, (j + 1) * HEAD_WIDTH)
+        for n, ref in enumerate((sk_ref, sv_ref, tk_ref, tv_ref)):
+            kv_out[j, :, :, n * HEAD_WIDTH : (n + 1) * HEAD_WIDTH] = ref[:, columns].reshape(
+                per, half, HEAD_WIDTH
+            )
+
+    def slot(ref, g):
+        return ref.at[pl.ds(g * per, per)]
+
+    def kv_copy(t):
+        head = t * 2 // share
+        return remote(
+            kv_out.at[head], slot(kv_in, me), kvs.at[t], kvr.at[mine], {"seq": t * 2 + side}
+        )
+
+    def kv_arrival(t):
+        return remote(
+            kv_out.at[0], slot(kv_in, t * 2 + side), kvs.at[t], kvr.at[t], {"seq": t * 2 + side}
+        )
+
+    def kv_forward(t):
+        block = slot(kv_in, t * 2 + side)
+        return remote(block, block, fs.at[t], fr.at[t], {"seq": partner})
+
+    def kv_forwarded(t):
+        block = slot(kv_in, t * 2 + 1 - side)
+        return remote(block, block, fs.at[t], fr.at[t], {"seq": partner})
+
+    def q_copy(out, into, send, receive, g):
+        return remote(out.at[g], slot(into, me), send.at[g], receive.at[me], {"seq": g})
+
+    def q_arrival(out, into, send, receive, g):
+        return remote(out.at[g], slot(into, g), send.at[g], receive.at[g], {"seq": g})
+
+    for t in peers:
+        kv_copy(t).start()
+    kv_in[pl.ds(me * per, per)] = kv_out[me // share]
+    kv_forward(mine).start()
+    for g in range(groups):
+        sq_out[g] = sq_ref[:, g * ws : (g + 1) * ws].reshape(per, half, ws)
+    for g in everyone:
+        q_copy(sq_out, sq_in, sqs, sqr, g).start()
+    sq_in[pl.ds(me * per, per)] = sq_out[me]
+    for g in range(groups):
+        tq_out[g] = tq_ref[:, g * wt : (g + 1) * wt].reshape(per, half, wt)
+    for g in everyone:
+        q_copy(tq_out, tq_in, tqs, tqr, g).start()
+    tq_in[pl.ds(me * per, per)] = tq_out[me]
+    for t in peers:
+        kv_arrival(t).wait_recv()
+        kv_forward(t).start()
+    for t in range(chain):
+        kv_forwarded(t).wait_recv()
+    for g in everyone:
+        q_arrival(sq_out, sq_in, sqs, sqr, g).wait_recv()
+    length = halves * half
+    queries = sq_in[...].reshape(length, ws)
+    pairs = kv_in[...].reshape(length, 4 * HEAD_WIDTH)
+    for at in range(0, length, PICKED):
+        rows = slice(at, at + PICKED)
+        held_ref[rows, :ws] = reordered(inverse_ref[rows, :], queries)
+        moved = reordered(inverse_ref[rows, :], pairs)
+        held_ref[rows, ws:] = moved[:, : 2 * HEAD_WIDTH]
+        t_held[rows, wt:] = moved[:, 2 * HEAD_WIDTH :]
+    student_blocks(ws // HEAD_WIDTH, held_ref, col_ref, row_ref, so_ref, prob_ref)
+    for g in everyone:
+        q_arrival(tq_out, tq_in, tqs, tqr, g).wait_recv()
+    queries = tq_in[...].reshape(length, wt)
+    for at in range(0, length, PICKED):
+        rows = slice(at, at + PICKED)
+        t_held[rows, :wt] = reordered(inverse_ref[rows, :], queries)
+    teacher_blocks(wt // HEAD_WIDTH, t_held, col_ref, row_ref, to_ref)
+    for t in peers:
+        kv_copy(t).wait_send()
+    for t in range(chain):
+        kv_forward(t).wait_send()
+    for g in everyone:
+        q_copy(sq_out, sq_in, sqs, sqr, g).wait_send()
+        q_copy(tq_out, tq_in, tqs, tqr, g).wait_send()
+
+
+def back_kernel(
+    groups, halves, reps, order_ref, held_ref, prob_ref, so_ref, grad_ref, dw_ref,
+    dq_ref, dk_ref, dv_ref, dwo_ref,
+    done, out, into, dw_in, dk, dv, qs, qr, ws_sem, wr_sem,
+):
+    me, rep = lax.axis_index("seq"), lax.axis_index("rep")
     length = held_ref.shape[0]
-    half = length // halves
-    at = heads * HEAD_WIDTH
+    half, per = length // halves, halves // groups
+    tokens = per * half
+    at = so_ref.shape[1]
+    heads = at // HEAD_WIDTH
     scaling = 1.0 / math.sqrt(HEAD_WIDTH)
+    everyone = [lax.rem(me + d, groups) for d in range(1, groups)]
+    mates = [lax.rem(rep + d, reps) for d in range(1, reps)]
+    greet(everyone, mates)
+
+    def weight_copy(r):
+        return remote(dw_ref.at[r], dw_in.at[rep], ws_sem.at[r], wr_sem.at[rep], {"rep": r})
+
+    def weight_arrival(r):
+        return remote(dw_ref.at[r], dw_in.at[r], ws_sem.at[r], wr_sem.at[r], {"rep": r})
+
+    def copy(g):
+        return remote(
+            out.at[pl.ds(g * per, per)], into.at[me], qs.at[g], qr.at[me], {"seq": g}
+        )
+
+    def arrival(g):
+        return remote(out.at[pl.ds(g * per, per)], into.at[g], qs.at[g], qr.at[g], {"seq": g})
+
+    for r in mates:
+        weight_copy(r).start()
     dk[...] = jnp.zeros_like(dk)
     dv[...] = jnp.zeros_like(dv)
     for i, (first, low, high) in enumerate(windows(length)):
@@ -128,70 +274,119 @@
         dv[low:high, :] += lax.dot_general(probs, grads, TN, preferred_element_type=jnp.float32)
     done[:, at : at + HEAD_WIDTH] = (dk[...] * scaling).astype(jnp.bfloat16)
     done[:, at + HEAD_WIDTH : at + 2 * HEAD_WIDTH] = dv[...].astype(jnp.bfloat16)
-    for place in range(halves):
-        start = pl.multiple_of(order_ref[place] * half, half)
-        out_ref[place * half : (place + 1) * half, :] = done[pl.ds(start, half), :]
-
-
-SMEM = pl.BlockSpec(memory_space=pltpu.SMEM)
+    everything = done[...]
+    count = PICKED // half
+    for top in range(0, length, PICKED):
+        moved = reordered(order_ref[top : top + PICKED, :], everything)
+        out[top // half : top // half + count] = moved.reshape(count, half, moved.shape[1])
+    for g in everyone:
+        copy(g).start()
+    into[me] = out[pl.ds(me * per, per)]
+    for r in mates:
+        weight_arrival(r).wait_recv()
+    total = dw_ref[rep].astype(jnp.float32)
+    for r in mates:
+        total = total + dw_in[r].astype(jnp.float32)
+    dwo_ref[...] = total
+    for g in everyone:
+        arrival(g).wait_recv()
+    for g in range(groups):
+        dq_ref[:, g * at : (g + 1) * at] = into[g, :, :, :at].reshape(tokens, at)
+    kv_heads = dk_ref.shape[1] // HEAD_WIDTH
+    share = groups // kv_heads
+    for j in range(kv_heads):
+        both = into[j * share, :, :, at:].astype(jnp.float32)
+        for g in range(j * share + 1, (j + 1) * share):
+            both = both + into[g, :, :, at:].astype(jnp.float32)
+        both = both.astype(jnp.bfloat16).reshape(tokens, 2 * HEAD_WIDTH)
+        dk_ref[:, j * HEAD_WIDTH : (j + 1) * HEAD_WIDTH] = both[:, :HEAD_WIDTH]
+        dv_ref[:, j * HEAD_WIDTH : (j + 1) * HEAD_WIDTH] = both[:, HEAD_WIDTH:]
+    for r in mates:
+        weight_copy(r).wait_send()
+    for g in everyone:
+        copy(g).wait_send()
+
+
 VMEM = pl.BlockSpec(memory_space=pltpu.VMEM)
-PARAMS = pltpu.CompilerParams(vmem_limit_bytes=VMEM_LIMIT)
+
+
+def remote_params(number):
+    return pltpu.CompilerParams(
+        collective_id=number, has_side_effects=True, vmem_limit_bytes=VMEM_LIMIT
+    )
 
 
 def shape(dims, dtype=jnp.bfloat16):
     return jax.ShapeDtypeStruct(dims, dtype)
 
 
-def teacher_attention(heads, halves, inverse, pack, col, row):
-    length, wide = pack.shape
-    flops = 4 * heads * HEAD_WIDTH * length * (length // 4 + ROWS)
+def forward(groups, halves, inverse, t_query, t_key, t_value, s_query, s_key, s_value, col, row):
+    length = col.shape[0]
+    tokens = t_query.shape[0]
+    half, per = length // halves, halves // groups
+    ws, wt = s_query.shape[1] // groups, t_query.shape[1] // groups
+    kv_heads = s_key.shape[1] // HEAD_WIDTH
+    flops = 4 * (ws + wt) * length * (length // 4 + ROWS)
+    bf16 = jnp.bfloat16
+    sems = pltpu.SemaphoreType.DMA
     return pl.pallas_call(
-        functools.partial(teacher_kernel, heads, halves),
-        out_shape=shape((length, heads * HEAD_WIDTH)),
-        in_specs=[SMEM, VMEM, VMEM, VMEM],
-        out_specs=VMEM,
-        scratch_shapes=[pltpu.VMEM((length, wide), jnp.bfloat16)],
-        compiler_params=PARAMS,
-        cost_estimate=pl.CostEstimate(flops=flops, bytes_accessed=4 << 20, transcendentals=flops // 512),
-        name="teacher_attention",
-    )(inverse, pack, col, row)
-
-
-def student_attention(heads, halves, inverse, pack, col, row):
-    length, wide = pack.shape
-    flops = 4 * heads * HEAD_WIDTH * length * (length // 4 + ROWS)
+        functools.partial(forward_kernel, groups, halves),
+        out_shape=(
+            shape((length, ws)),
+            shape((length, ws + 2 * HEAD_WIDTH)),
+            shape((length // ROWS, ws // HEAD_WIDTH * ROWS, length // 4 + ROWS)),
+            shape((length, wt)),
+        ),
+        in_specs=[VMEM] * 9,
+        out_specs=(VMEM,) * 4,
+        scratch_shapes=[
+            pltpu.VMEM((groups, per, half, ws), bf16),
+            pltpu.VMEM((halves, half, ws), bf16),
+            pltpu.VMEM((groups, per, half, wt), bf16),
+            pltpu.VMEM((halves, half, wt), bf16),
+            pltpu.VMEM((kv_heads, per, half, 4 * HEAD_WIDTH), bf16),
+            pltpu.VMEM((halves, half, 4 * HEAD_WIDTH), bf16),
+            pltpu.VMEM((length, wt + 2 * HEAD_WIDTH), bf16),
+        ]
+        + [sems((groups,))] * 4
+        + [sems((groups // 2,))] * 4,
+        compiler_params=remote_params(1),
+        cost_estimate=pl.CostEstimate(flops=flops, bytes_accessed=6 << 20, transcendentals=flops // 512),
+        name="forward",
+    )(inverse, t_query, t_key, t_value, s_query, s_key, s_value, col, row)
+
+
+def backward(groups, halves, order, held, probs, out, grad, d_weight, kv_columns):
+    length, wide = held.shape
+    half, per, tokens = length // halves, halves // groups, length // groups
+    ws = out.shape[1]
+    reps, _, columns = d_weight.shape
+    flops = 10 * ws * length * (length // 4 + ROWS)
+    bf16 = jnp.bfloat16
+    sems = pltpu.SemaphoreType.DMA
     return pl.pallas_call(
-        functools.partial(student_kernel, heads, halves),
+        functools.partial(back_kernel, groups, halves, reps),
         out_shape=(
-            shape((length, heads * HEAD_WIDTH)),
-            shape((length, wide)),
-            shape((length // ROWS, heads * ROWS, length // 4 + ROWS)),
+            shape((tokens, ws * groups)),
+            shape((tokens, kv_columns)),
+            shape((tokens, kv_columns)),
+            shape((ws, columns), jnp.float32),
         ),
-        in_specs=[SMEM, VMEM, VMEM, VMEM],
-        out_specs=(VMEM, VMEM, VMEM),
-        compiler_params=PARAMS,
-        cost_estimate=pl.CostEstimate(flops=flops, bytes_accessed=6 << 20, transcendentals=flops // 512),
-        name="student_attention",
-    )(inverse, pack, col, row)
-
-
-def student_backward(heads, halves, order, held, probs, out, grad):
-    length, wide = held.shape
-    flops = 10 * heads * HEAD_WIDTH * length * (length // 4 + ROWS)
-    return pl.pallas_call(
-        functools.partial(back_kernel, heads, halves),
-        out_shape=shape((length, wide)),
-        in_specs=[SMEM, VMEM, VMEM, VMEM, VMEM],
-        out_specs=VMEM,
+        in_specs=[VMEM] * 6,
+        out_specs=(VMEM,) * 4,
         scratch_shapes=[
-            pltpu.VMEM((length, wide), jnp.bfloat16),
+            pltpu.VMEM((length, wide), bf16),
+            pltpu.VMEM((halves, half, wide), bf16),
+            pltpu.VMEM((groups, per, half, wide), bf16),
+            pltpu.VMEM((reps, ws, columns), bf16),
             pltpu.VMEM((length, HEAD_WIDTH), jnp.float32),
             pltpu.VMEM((length, HEAD_WIDTH), jnp.float32),
+            sems((groups,)), sems((groups,)), sems((reps,)), sems((reps,)),
         ],
-        compiler_params=PARAMS,
+        compiler_params=remote_params(2),
         cost_estimate=pl.CostEstimate(flops=flops, bytes_accessed=6 << 20, transcendentals=0),
-        name="student_backward",
-    )(order, held, probs, out, grad)
+        name="backward",
+    )(order, held, probs, out, grad, d_weight)
 
 
 def exchange_kernel(
@@ -208,19 +403,8 @@
     partner = {"seq": mine * 2 + other}
     peers = [lax.rem(mine + d, chain) for d in range(1, chain)]
 
-    barrier = pltpu.get_barrier_semaphore()
-    pl.semaphore_signal(barrier, inc=1, device_id=partner, device_id_type=pl.DeviceIdType.MESH)
-    for peer in peers:
-        pl.semaphore_signal(
-            barrier, inc=1, device_id={"seq": peer * 2 + side}, device_id_type=pl.DeviceIdType.MESH
-        )
-    pl.semaphore_wait(barrier, chain)
-
-    def copy(source, target, send, receive, device):
-        return pltpu.make_async_remote_copy(
-            src_ref=source, dst_ref=target, send_sem=send, recv_sem=receive,
-            device_id=device, device_id_type=pl.DeviceIdType.MESH,
-        )
+    greet([mine * 2 + other] + [peer * 2 + side for peer in peers])
+    copy = remote
 
     def pair_copy(c, t):
         return copy(pair_out.at[c, t], pair_in.at[c, t], ps.at[c, t], pr.at[c, t], partner)
@@ -308,7 +492,9 @@
         else:
             loss_ref[...] += squares
             total[...] += d_attn
-        dw_ref[:, columns] = lax.dot_general(
+        share = dw_ref.shape[2]
+        at = c * width % share
+        dw_ref[c * width // share, :, at : at + width] = lax.dot_general(
             so_ref[...].reshape(length, so_ref.shape[3]), block, TN,
             preferred_element_type=jnp.float32,
         ).astype(jnp.bfloat16)
@@ -328,7 +514,7 @@
             grad_copy(c, peer).wait_send()
 
 
-def exchange(groups, chunks, student_out, teacher_out, student_wo, projection):
+def exchange(groups, reps, chunks, student_out, teacher_out, student_wo, projection):
     length, ws = student_out.shape
     wt = teacher_out.shape[1]
     chain, tokens = groups // 2, length // groups
@@ -339,7 +525,8 @@
     return pl.pallas_call(
         functools.partial(exchange_kernel, chain, chunks),
         out_shape=(
-            shape((length, ws)), shape((ws, columns)), shape((1, width), jnp.float32),
+            shape((length, ws)), shape((reps, ws, columns // reps)),
+            shape((1, width), jnp.float32),
         ),
         in_specs=[VMEM] * 4,
         out_specs=(VMEM, VMEM, VMEM),
@@ -349,9 +536,7 @@
             pltpu.VMEM((length, ws), jnp.float32),
         ]
         + [sems] * 8,
-        compiler_params=pltpu.CompilerParams(
-            collective_id=0, has_side_effects=True, vmem_limit_bytes=VMEM_LIMIT
-        ),
+        compiler_params=remote_params(0),
         cost_estimate=pl.CostEstimate(
             flops=2 * length * columns * (3 * ws + wt), bytes_accessed=8 << 20, transcendentals=0
         ),
@@ -360,16 +545,6 @@
         student_out.reshape(chain, 2, tokens, ws), teacher_out.reshape(chain, 2, tokens, wt),
         student_wo, projection,
     )
-
-
-def by_group(rows, groups):
-    tokens, wide = rows.shape
-    return jnp.transpose(rows.reshape(tokens, groups, wide // groups), (1, 0, 2))
-
-
-def by_shared_head(rows, groups):
-    heads = rows.shape[1] // HEAD_WIDTH
-    return jnp.repeat(by_group(rows, heads), groups // heads, axis=0)
 
 
 def shards(
@@ -384,72 +559,30 @@
     doc_ids,
     span_order,
 ):
-    groups = lax.axis_size("seq")
-    tokens = t_query.shape[1]
-    length = tokens * groups
+    groups, reps = lax.axis_size("seq"), lax.axis_size("rep")
+    length = t_query.shape[1] * groups
     halves = span_order.shape[1]
-    t_local = t_query.shape[2] // HEAD_WIDTH // groups
-    s_heads = s_query.shape[2] // HEAD_WIDTH
-    s_local = s_heads // groups
-    s_kv = s_key.shape[2] // HEAD_WIDTH
     order = span_order[0]
     places = jnp.arange(halves, dtype=jnp.int32)
     inverse = jnp.sum(
         jnp.where(order[None, :] == places[:, None], places[None, :], 0), axis=1, dtype=jnp.int32
     )
-    col = doc_ids.reshape(length, 1)
-    row = doc_ids.reshape(1, length)
-
-    s_pack = jnp.concatenate(
-        [
-            by_group(s_query[0], groups),
-            by_shared_head(s_key[0], groups),
-            by_shared_head(student_value[0], groups),
-        ],
-        axis=2,
-    )
-    t_pack = jnp.concatenate(
-        [
-            by_group(t_query[0], groups),
-            by_shared_head(t_key[0], groups),
-            by_shared_head(t_value[0], groups),
-        ],
-        axis=2,
-    )
-    s_rows = lax.all_to_all(s_pack, "seq", split_axis=0, concat_axis=0, tiled=True)
-    t_rows = lax.all_to_all(t_pack, "seq", split_axis=0, concat_axis=0, tiled=True)
-    s_rows = s_rows.reshape(length, s_pack.shape[2])
-    t_rows = t_rows.reshape(length, t_pack.shape[2])
-    student_out, held, probs = student_attention(s_local, halves, inverse, s_rows, col, row)
-    teacher_out = teacher_attention(t_local, halves, inverse, t_rows, col, row)
-
-    width_all = student_wo.shape[1]
+    half = length // halves
+    offsets = jnp.arange(half, dtype=jnp.int32)
+    inverse = (inverse[:, None] * half + offsets[None, :]).reshape(length, 1)
+    order = (order[:, None] * half + offsets[None, :]).reshape(length, 1)
+    student_out, held, probs, teacher_out = forward(
+        groups, halves, inverse, t_query[0], t_key[0], t_value[0], s_query[0], s_key[0], student_value[0],
+        doc_ids.reshape(length, 1), doc_ids.reshape(1, length),
+    )
     d_attn, d_weight, squares = exchange(
-        groups, CHUNKS, student_out, teacher_out, student_wo, projection
-    )
-    seq_loss = (jnp.sum(squares) / (length * width_all)).reshape(1)
-    weight_share = lax.psum_scatter(
-        d_weight, "rep", scatter_dimension=1, tiled=True
-    ).astype(jnp.float32)
-    back = student_backward(s_local, halves, order, held, probs, student_out, d_attn)
-    back = lax.all_to_all(
-        back.reshape(groups, tokens, back.shape[1]), "seq", split_axis=0, concat_axis=0, tiled=True
-    )
-    at = s_local * HEAD_WIDTH
-    d_query = jnp.transpose(back[:, :, :at], (1, 0, 2)).reshape(1, tokens, s_heads * HEAD_WIDTH)
-
-    def merge(parts):
-        summed = parts.reshape(s_kv, groups // s_kv, tokens, HEAD_WIDTH).astype(jnp.float32)
-        summed = summed.sum(axis=1).astype(jnp.bfloat16)
-        return jnp.transpose(summed, (1, 0, 2)).reshape(1, tokens, s_kv * HEAD_WIDTH)
-
-    return (
-        seq_loss,
-        weight_share,
-        d_query,
-        merge(back[:, :, at : at + HEAD_WIDTH]),
-        merge(back[:, :, at + HEAD_WIDTH :]),
-    )
+        groups, reps, CHUNKS, student_out, teacher_out, student_wo, projection
+    )
+    seq_loss = (jnp.sum(squares) / (length * student_wo.shape[1])).reshape(1)
+    d_query, d_key, d_value, d_wo = backward(
+        groups, halves, order, held, probs, student_out, d_attn, d_weight, s_key.shape[2]
+    )
+    return (seq_loss, d_wo, d_query[None], d_key[None], d_value[None])
 
 
 def solution(mesh):

time: 250 us -> 215 us (0.86)
  waiting for transfers between devices: 75.4 us -> 0 us
  Pallas kernels: 124 us -> 197 us
  starting transfers between devices: 17.4 us -> 0 us
  between operations: 16.1 us -> 2.53 us
  other arithmetic: 4.95 us -> 1.53 us
  local copies, waits for them, and re-layouts: 10.5 us -> 13.1 us
    pallas_call x3 -> x2, Pallas kernels: 12 us -> 91.7 us  [the longest x1 55.5 us: forward(): pl.pallas_call(functools.partial(forward_kernel, groups, halves), out_sha...]
    all_to_all x3 -> x0, waiting for transfers between devices: 69.1 us -> none  [the longest x1 27.3 us: shards(): lax.all_to_all(t_pack, 'seq', split_axis=0, concat_axis=0, tiled=True)]
    all_to_all x3 -> x0, starting transfers between devices: 17.4 us -> none  [the longest x1 6.35 us: shards(): lax.all_to_all(t_pack, 'seq', split_axis=0, concat_axis=0, tiled=True)]
    pallas_call x1, Pallas kernels: 112 us -> 106 us  [exchange(): pl.pallas_call(functools.partial(exchange_kernel, chain, chunks), out_sha...]
    reduce_scatter x1 -> x0, waiting for transfers between devices: 5.65 us -> none  [shards(): lax.psum_scatter(d_weight, 'rep', scatter_dimension=1, tiled=True)]
    unnamed x28 -> x26, local copies, waits for them, and re-layouts: 6.06 us -> 11.3 us
  transfers between devices with their start and end apart: 4 -> 0, of which waited for: 4 -> 0; matrix products, arithmetic and copies ran while one was open for 3% -> 0% of each run, Pallas kernels for 2% -> 0%
where the time goes in v3:
time: 215 us; the launch traced here: 214 us
  Pallas kernels  197 us (92%)
  local copies, waits for them, and re-layouts  13.1 us (6%)
  between operations  2.53 us (1%)
    pallas_call x1, Pallas kernels, exchange(): pl.pallas_call(functools.partial(exchange_kernel, chain, chunks), out_sha...  106 us
    pallas_call x1, Pallas kernels, forward(): pl.pallas_call(functools.partial(forward_kernel, groups, halves), out_sha...  55.5 us
    pallas_call x1, Pallas kernels, backward(): pl.pallas_call(functools.partial(back_kernel, groups, halves, reps), out_...  36.2 us
    unnamed x26, local copies, waits for them, and re-layouts  11.3 us

profile of v3, /device:TPU:11, one launch (start us, length us, event | category | flops | bytes accessed | tf_op | source)
XLA Modules:
  0.0 214.4 jit_solution(7363837872803674309)
XLA Ops:
  0.6 0.8 select_reduce_fusion
  1.4 0.1 iota_add_fusion.1
  1.5 0.5 add.54.inverse_ref
  2.0 0.9 copy.19.col_ref
  2.9 0.0 copy-start.2
  2.9 0.7 copy-done.2
  3.6 0.0 copy-start.3
  3.6 1.2 copy-done.3
  4.8 0.0 copy-start.5
  4.8 1.0 copy-done.5
  5.8 0.0 copy-start.6
  5.8 0.9 copy-done.6
  6.7 0.0 copy-start.7
  6.7 0.9 copy-done.7
  7.6 0.0 copy-start.8
  7.6 0.9 copy-done.8
  8.5 0.0 copy-start.9
  8.6 0.9 copy-done.9
  9.5 0.0 copy-start.4
  9.5 55.5 %forward.1 = (bf16[1024,256]{1,0:T(8,128)(2,1)S(1)}, bf16[1024,512]{1,0:T(8,128)(2,1)S(1)}, bf16[8,256,384]{2,1,0:T(8,128)(2,1)}, bf16[1024,512]{1,0:T(8,128)(2,1)S(1)}) custom-call(s32[1024,1]{1,0:T(8,128)S(1)} %add.54.inverse_ref, bf16[128,4096]{1,0:T(8,128)(2,1)S(1)} %bitcast.20, bf16[128,512]{1,0:T(8,128)(2,1)S(1)} %bitcast.22, ...), custom_call_target="tpu_custom_call" | custom-call | flops 1207959552 | bytes 6291456 | tf_op jit(solution)/shard_map/forward/pallas_call | solution.py:332
  64.9 0.0 copy-done.4
  64.9 0.0 copy-start.10
  64.9 105.5 %exchange.1 = (bf16[1024,256]{1,0:T(8,128)(2,1)S(1)}, bf16[4,256,512]{2,1,0:T(8,128)(2,1)S(1)}, f32[1,128]{1,0:T(1,128)S(1)}) custom-call(bf16[4,2,128,256]{3,2,1,0:T(8,128)(2,1)S(1)} %bitcast.15, bf16[4,2,128,512]{3,2,1,0:T(8,128)(2,1)S(1)} %bitcast.26, bf16[256,2048]{1,0:T(8,128)(2,1)S(1)} %copy-done.4, bf16[512,2048]{1,0:T(8,128)(2,1)} %pj_ref.1), custom_call_target="tpu_custom_call" | custom-call | flops 5368709120 | bytes 8388608 | tf_op jit(solution)/shard_map/exchange/pallas_call | solution.py:525
  170.5 0.0 copy-start
  170.5 0.8 copy-done
  171.3 0.6 reduce_sum.19
  172.5 0.0 copy-done.10
  172.5 0.1 iota_add_fusion
  172.6 0.5 add.55.order_ref
  173.1 0.0 copy-start.1
  173.1 1.0 copy-done.1
  174.1 36.2 %backward.1 = (bf16[128,2048]{1,0:T(8,128)(2,1)S(1)}, bf16[128,512]{1,0:T(8,128)(2,1)S(1)}, bf16[128,512]{1,0:T(8,128)(2,1)S(1)}, f32[256,512]{1,0:T(8,128)S(1)}) custom-call(s32[1024,1]{1,0:T(8,128)S(1)} %add.55.order_ref, bf16[1024,512]{1,0:T(8,128)(2,1)S(1)} %get-tuple-element.19.held_ref, bf16[8,256,384]{2,1,0:T(8,128)(2,1)} %get-tuple-element.20.prob_ref, ...), custom_call_target="tpu_custom_call" | custom-call | flops 1006632960 | bytes 6291456 | tf_op jit(solution)/shard_map/backward/pallas_call | solution.py:367
  210.4 0.8 copy.25
  211.2 0.8 copy.26
  212.0 0.7 copy.27
  212.6 0.7 copy.28
  (2 shorter events, 0.0 us)
Async XLA Ops:
  2.9 0.7 copy-start.2
  3.6 1.2 copy-start.3
  4.8 1.0 copy-start.5
  5.8 0.9 copy-start.6
  6.7 0.9 copy-start.7
  7.6 0.9 copy-start.8
  8.5 0.9 copy-start.9
  9.5 55.5 %copy-start.4 = (bf16[256,2048]{1,0:T(8,128)(2,1)S(1)}, bf16[256,2048]{1,0:T(8,128)(2,1)}, u32[]{:S(2)}) copy-start(bf16[256,2048]{1,0:T(8,128)(2,1)} %wo_ref.1) | copy-start | bytes 3145732
  64.9 107.6 %copy-start.10 = (s32[1,16]{1,0:T(1,128)S(1)}, s32[1,16]{1,0:T(1,128)}, u32[]{:S(2)}) copy-start(s32[1,16]{1,0:T(1,128)} %param.19) | copy-start | bytes 196
  170.5 0.8 copy-start
  173.1 1.0 copy-start.1

commit v4 on v3

--- a/solution.py
+++ b/solution.py
@@ -14,6 +14,7 @@
 CHUNKS = 16
 MASKED = -1e30
 VMEM_LIMIT = 48 * 1024 * 1024
+FORWARD_LIMIT = 62 * 1024 * 1024
 NT = (((1,), (1,)), ((), ()))
 TN = (((0,), (0,)), ((), ()))
 
@@ -86,10 +87,18 @@
             ]
 
 
-def reordered(source_rows, source):
-    count, length = source_rows.shape[0], source.shape[0]
-    places = lax.broadcasted_iota(jnp.int32, (count, length), 1)
-    picks = jnp.where(source_rows == places, 1.0, 0.0).astype(jnp.bfloat16)
+def reordered(spans_ref, top, half, source):
+    length = source.shape[0]
+    offset = lax.broadcasted_iota(jnp.int32, (half, length), 1) - lax.broadcasted_iota(
+        jnp.int32, (half, length), 0
+    )
+    picks = jnp.concatenate(
+        [
+            jnp.where(offset == spans_ref[place] * half, 1.0, 0.0).astype(jnp.bfloat16)
+            for place in range(top // half, (top + PICKED) // half)
+        ],
+        axis=0,
+    )
     return jnp.dot(picks, source, preferred_element_type=jnp.float32).astype(jnp.bfloat16)
 
 
@@ -113,8 +122,9 @@
 
 
 def forward_kernel(
-    groups, halves, inverse_ref, tq_ref, tk_ref, tv_ref, sq_ref, sk_ref, sv_ref, col_ref, row_ref,
+    groups, halves, inverse_ref, tq_hbm, tk_hbm, tv_hbm, sq_hbm, sk_hbm, sv_hbm, col_ref, row_ref,
     so_ref, held_ref, prob_ref, to_ref,
+    tq_ref, tk_ref, tv_ref, sq_ref, sk_ref, sv_ref, local,
     sq_out, sq_in, tq_out, tq_in, kv_out, kv_in, t_held,
     sqs, sqr, tqs, tqr, kvs, kvr, fs, fr,
 ):
@@ -128,8 +138,21 @@
     share = groups // kv_heads
     everyone = [lax.rem(me + d, groups) for d in range(1, groups)]
     peers = [lax.rem(mine + d, chain) for d in range(1, chain)]
+    loads = [
+        pltpu.make_async_copy(source, target, local.at[n])
+        for n, (source, target) in enumerate(
+            (
+                (sk_hbm, sk_ref), (sv_hbm, sv_ref), (tk_hbm, tk_ref), (tv_hbm, tv_ref),
+                (sq_hbm, sq_ref), (tq_hbm, tq_ref),
+            )
+        )
+    ]
+    for load in loads:
+        load.start()
     greet(everyone)
 
+    for load in loads:
+        load.wait()
     for j in range(kv_heads):
         columns = slice(j * HEAD_WIDTH, (j + 1) * HEAD_WIDTH)
         for n, ref in enumerate((sk_ref, sv_ref, tk_ref, tv_ref)):
@@ -191,8 +214,8 @@
     pairs = kv_in[...].reshape(length, 4 * HEAD_WIDTH)
     for at in range(0, length, PICKED):
         rows = slice(at, at + PICKED)
-        held_ref[rows, :ws] = reordered(inverse_ref[rows, :], queries)
-        moved = reordered(inverse_ref[rows, :], pairs)
+        held_ref[rows, :ws] = reordered(inverse_ref, at, half, queries)
+        moved = reordered(inverse_ref, at, half, pairs)
         held_ref[rows, ws:] = moved[:, : 2 * HEAD_WIDTH]
         t_held[rows, wt:] = moved[:, 2 * HEAD_WIDTH :]
     student_blocks(ws // HEAD_WIDTH, held_ref, col_ref, row_ref, so_ref, prob_ref)
@@ -201,7 +224,7 @@
     queries = tq_in[...].reshape(length, wt)
     for at in range(0, length, PICKED):
         rows = slice(at, at + PICKED)
-        t_held[rows, :wt] = reordered(inverse_ref[rows, :], queries)
+        t_held[rows, :wt] = reordered(inverse_ref, at, half, queries)
     teacher_blocks(wt // HEAD_WIDTH, t_held, col_ref, row_ref, to_ref)
     for t in peers:
         kv_copy(t).wait_send()
@@ -277,7 +300,7 @@
     everything = done[...]
     count = PICKED // half
     for top in range(0, length, PICKED):
-        moved = reordered(order_ref[top : top + PICKED, :], everything)
+        moved = reordered(order_ref, top, half, everything)
         out[top // half : top // half + count] = moved.reshape(count, half, moved.shape[1])
     for g in everyone:
         copy(g).start()
@@ -307,12 +330,13 @@
         copy(g).wait_send()
 
 
+SMEM = pl.BlockSpec(memory_space=pltpu.SMEM)
 VMEM = pl.BlockSpec(memory_space=pltpu.VMEM)
 
 
-def remote_params(number):
+def remote_params(number, limit=VMEM_LIMIT):
     return pltpu.CompilerParams(
-        collective_id=number, has_side_effects=True, vmem_limit_bytes=VMEM_LIMIT
+        collective_id=number, has_side_effects=True, vmem_limit_bytes=limit
     )
 
 
@@ -337,9 +361,14 @@
             shape((length // ROWS, ws // HEAD_WIDTH * ROWS, length // 4 + ROWS)),
             shape((length, wt)),
         ),
-        in_specs=[VMEM] * 9,
+        in_specs=[SMEM] + [pl.BlockSpec(memory_space=pltpu.HBM)] * 6 + [VMEM] * 2,
         out_specs=(VMEM,) * 4,
         scratch_shapes=[
+            pltpu.VMEM(array.shape, bf16)
+            for array in (t_query, t_key, t_value, s_query, s_key, s_value)
+        ]
+        + [
+            sems((6,)),
             pltpu.VMEM((groups, per, half, ws), bf16),
             pltpu.VMEM((halves, half, ws), bf16),
             pltpu.VMEM((groups, per, half, wt), bf16),
@@ -350,7 +379,7 @@
         ]
         + [sems((groups,))] * 4
         + [sems((groups // 2,))] * 4,
-        compiler_params=remote_params(1),
+        compiler_params=remote_params(1, FORWARD_LIMIT),
         cost_estimate=pl.CostEstimate(flops=flops, bytes_accessed=6 << 20, transcendentals=flops // 512),
         name="forward",
     )(inverse, t_query, t_key, t_value, s_query, s_key, s_value, col, row)
@@ -372,7 +401,7 @@
             shape((tokens, kv_columns)),
             shape((ws, columns), jnp.float32),
         ),
-        in_specs=[VMEM] * 6,
+        in_specs=[SMEM] + [VMEM] * 5,
         out_specs=(VMEM,) * 4,
         scratch_shapes=[
             pltpu.VMEM((length, wide), bf16),
@@ -499,8 +528,8 @@
             preferred_element_type=jnp.float32,
         ).astype(jnp.bfloat16)
 
-    stages = ((first_stage, 0), (second_stage, 2), (third_stage, 3), (fourth_stage, 4), (fifth_stage, 5))
-    for step in range(chunks + 5):
+    stages = ((first_stage, 0), (second_stage, 3), (third_stage, 4), (fourth_stage, 5), (fifth_stage, 7))
+    for step in range(chunks + 7):
         for stage, lag in stages:
             if 0 <= step - lag < chunks:
                 stage(step - lag)
@@ -567,10 +596,6 @@
     inverse = jnp.sum(
         jnp.where(order[None, :] == places[:, None], places[None, :], 0), axis=1, dtype=jnp.int32
     )
-    half = length // halves
-    offsets = jnp.arange(half, dtype=jnp.int32)
-    inverse = (inverse[:, None] * half + offsets[None, :]).reshape(length, 1)
-    order = (order[:, None] * half + offsets[None, :]).reshape(length, 1)
     student_out, held, probs, teacher_out = forward(
         groups, halves, inverse, t_query[0], t_key[0], t_value[0], s_query[0], s_key[0], student_value[0],
         doc_ids.reshape(length, 1), doc_ids.reshape(1, length),

time: 215 us -> 215 us (level)
  no operation moved by 1% of the time
where the time goes in v4:
time: 215 us
  Pallas kernels  198 us (92%)
  local copies, waits for them, and re-layouts  12.1 us (6%)
  between operations  2.51 us (1%)
    pallas_call x1, Pallas kernels, exchange(): pl.pallas_call(functools.partial(exchange_kernel, chain, chunks), out_sha...  105 us
    pallas_call x1, Pallas kernels, forward(): pl.pallas_call(functools.partial(forward_kernel, groups, halves), out_sha...  57 us
    pallas_call x1, Pallas kernels, backward(): pl.pallas_call(functools.partial(back_kernel, groups, halves, reps), out_...  35.9 us
    unnamed x26, local copies, waits for them, and re-layouts  10.4 us

profile of v4, /device:TPU:11, one launch (start us, length us, event | category | flops | bytes accessed | tf_op | source)
XLA Modules:
  0.0 214.7 jit_solution(6884920258135993651)
XLA Ops:
  0.6 1.3 select_reduce_fusion.inverse_ref
  1.9 1.7 copy.16.col_ref
  3.6 57.0 %forward.1 = (bf16[1024,256]{1,0:T(8,128)(2,1)}, bf16[1024,512]{1,0:T(8,128)(2,1)}, bf16[8,256,384]{2,1,0:T(8,128)(2,1)}, bf16[1024,512]{1,0:T(8,128)(2,1)}) custom-call(s32[16]{0:T(128)} %select_reduce_fusion.inverse_ref, bf16[128,4096]{1,0:T(8,128)(2,1)} %bitcast.22, bf16[128,512]{1,0:T(8,128)(2,1)} %bitcast.24, bf16[128,512]{1,0:T(8,128)(2,1)} %bitcast.25, ...), custom_call_target="tpu_custom_call" | custom-call | flops 1207959552 | bytes 6291456 | tf_op jit(solution)/shard_map/forward/pallas_call | solution.py:356
  60.6 0.0 copy-start.4
  60.6 1.0 copy-done.4
  61.7 0.0 copy-start.9
  61.7 1.2 copy-done.9
  62.9 0.0 copy-start.10
  62.9 1.2 copy-done.10
  64.1 0.0 copy-start
  64.1 0.0 copy-start.1
  64.1 0.0 copy-start.5
  64.1 0.0 copy-start.8
  64.1 105.2 %exchange.1 = (bf16[1024,256]{1,0:T(8,128)(2,1)S(1)}, bf16[4,256,512]{2,1,0:T(8,128)(2,1)S(1)}, f32[1,128]{1,0:T(1,128)S(1)}) custom-call(bf16[4,2,128,256]{3,2,1,0:T(8,128)(2,1)S(1)} %bitcast.14, bf16[4,2,128,512]{3,2,1,0:T(8,128)(2,1)S(1)} %bitcast.20, bf16[256,2048]{1,0:T(8,128)(2,1)S(1)} %copy-done.9, bf16[512,2048]{1,0:T(8,128)(2,1)} %pj_ref.1), custom_call_target="tpu_custom_call" | custom-call | flops 5368709120 | bytes 8388608 | tf_op jit(solution)/shard_map/exchange/pallas_call | solution.py:554
  169.4 0.0 copy-start.2
  169.4 1.0 copy-done.2
  170.3 0.0 copy-start.6
  170.3 0.8 copy-done.6
  171.1 0.6 reduce_sum.19
  172.4 0.0 copy-done
  172.4 0.0 copy-done.1
  172.4 0.0 copy-done.5
  172.4 0.0 copy-done.8
  172.4 0.0 copy-start.3
  172.4 1.2 copy-done.3
  173.6 0.0 copy-start.7
  173.7 1.0 copy-done.7
  174.7 35.9 %backward.1 = (bf16[128,2048]{1,0:T(8,128)(2,1)S(1)}, bf16[128,512]{1,0:T(8,128)(2,1)S(1)}, bf16[128,512]{1,0:T(8,128)(2,1)S(1)}, f32[256,512]{1,0:T(8,128)S(1)}) custom-call(s32[16]{0:T(128)S(1)} %bitcast.19, bf16[1024,512]{1,0:T(8,128)(2,1)S(1)} %copy-done.1, bf16[8,256,384]{2,1,0:T(8,128)(2,1)S(1)} %copy-done, bf16[1024,256]{1,0:T(8,128)(2,1)S(1)} %copy-done.5, ...), custom_call_target="tpu_custom_call" | custom-call | flops 1006632960 | bytes 6291456 | tf_op jit(solution)/shard_map/backward/pallas_call | solution.py:396
  210.6 0.8 copy.21
  211.4 0.8 copy.22
  212.2 0.7 copy.23
  212.9 0.7 copy.24
Async XLA Ops:
  60.6 1.0 copy-start.4
  61.7 1.2 copy-start.9
  62.9 1.2 copy-start.10
  64.1 108.3 %copy-start = (bf16[8,256,384]{2,1,0:T(8,128)(2,1)S(1)}, bf16[8,256,384]{2,1,0:T(8,128)(2,1)}, u32[]{:S(2)}) copy-start(bf16[8,256,384]{2,1,0:T(8,128)(2,1)} %get-tuple-element.20.prob_ref) | copy-start | bytes 4718596
  64.1 108.3 %copy-start.1 = (bf16[1024,512]{1,0:T(8,128)(2,1)S(1)}, bf16[1024,512]{1,0:T(8,128)(2,1)}, u32[]{:S(2)}) copy-start(bf16[1024,512]{1,0:T(8,128)(2,1)} %get-tuple-element.19.held_ref) | copy-start | bytes 3145732
  64.1 108.3 %copy-start.5 = (bf16[1024,256]{1,0:T(8,128)(2,1)S(1)}, bf16[1024,256]{1,0:T(8,128)(2,1)}, u32[]{:S(2)}) copy-start(bf16[1024,256]{1,0:T(8,128)(2,1)} %get-tuple-element.16.so_ref) | copy-start | bytes 1572868
  64.1 108.3 %copy-start.8 = (s32[1,16]{1,0:T(1,128)S(1)}, s32[1,16]{1,0:T(1,128)}, u32[]{:S(2)}) copy-start(s32[1,16]{1,0:T(1,128)} %param.19) | copy-start | bytes 196
  169.4 1.0 copy-start.2
  170.3 0.8 copy-start.6
  172.4 1.2 copy-start.3
  173.6 1.0 copy-start.7
